TPU v7x, 256 devices: a whole 4x4x8 slice. The times are simulated.
256 devices in a mesh: vseq: 32 (over x, y, z_lo), aseq: 8 (over z_hi, core).
Axes of the slice: x: 4, y: 4, z: 8 (z_hi: 4, z_lo: 2; z = z_hi * 2 + z_lo), core: 2. Of those that a mesh axis runs over, the one named last changes fastest.
Arguments:
- video_q: bfloat16 [12288, 24, 128], P(('vseq', 'aseq'))
- video_k: bfloat16 [12288, 24, 128], P(('vseq', 'aseq'))
- video_v: bfloat16 [12288, 24, 128], P(('vseq', 'aseq')), may hold values from -6 to 6
- audio_q: bfloat16 [2048, 24, 128], P(('vseq', 'aseq'))
- audio_k: bfloat16 [2048, 24, 128], P(('vseq', 'aseq'))
- audio_v: bfloat16 [2048, 24, 128], P(('vseq', 'aseq')), may hold values from -6 to 6
- video_x: bfloat16 [12288, 3072], P(('vseq', 'aseq')), may hold values from -3 to 3
- audio_x: bfloat16 [2048, 3072], P(('vseq', 'aseq')), may hold values from -3 to 3
- video_out_w: bfloat16 [3072, 3072], P('aseq'), may hold values from -0.4375 to 0.4375
- audio_out_w: bfloat16 [3072, 3072], P('aseq'), may hold values from -0.4375 to 0.4375
- video_gate_w: bfloat16 [256, 3072], replicated, may hold values from -0.375 to 0.375
- audio_gate_w: bfloat16 [256, 3072], replicated, may hold values from -0.375 to 0.375
- levels: int32 [8], replicated, may hold values from 0 to 999
- video_pos: int32 [8], replicated, may hold values from 0 to 166, as said below
- audio_pos: int32 [2048], P(('vseq', 'aseq')), may hold values from 0 to 197, as said below
Outputs:
- video_out: bfloat16 [12288, 3072], P(('vseq', 'aseq'))
- audio_out: bfloat16 [2048, 3072], P(('vseq', 'aseq'))
Inputs may be any that keep to these rules, and one draw needn't show every extreme that they name: `video_pos`: the first frame lies at 0; strictly increasing, consecutive frames 16 to 32 apart; the last frame lies at 166. `audio_pos`: non-decreasing; audio token f * 256 has exactly the position video_pos[f], and tokens f * 256 to (f + 1) * 256 - 1 lie before video_pos[f + 1] where that frame exists, and within 31 of video_pos[f].
All inputs are finite; a program needn't handle non-finite values.
Results may differ from a plain program's by a relative error of at most 0.014.
Values may be sent and summed in bfloat16 or wider, within the bound.
No kernel may reach another device: no remote copies, remote signals or barrier semaphores. Data moves between devices by JAX's collectives and lax.ppermute only.
A program may use at most 128 MiB of HBM per device.

v0:
```python
import math

import jax
import jax.numpy as jnp
from jax import lax
from jax.sharding import PartitionSpec as P

GRID_W = 32
LEVELS = 1000


flow_shift = 5.0


def rotate(values, place_t, place_h, place_w):
    head_dim = values.shape[-1]
    one_sixth = head_dim // 6
    first_width = head_dim - 4 * one_sixth
    outputs = []
    sections = (
        (0, first_width, place_t),
        (first_width, 2 * one_sixth, place_h),
        (first_width + 2 * one_sixth, 2 * one_sixth, place_w),
    )
    for start_col, width, places in sections:
        half_width = width // 2
        frequency = 10000.0 ** (-(jnp.arange(half_width, dtype=jnp.float32) * 2.0) / width)
        angles = places.astype(jnp.float32)[:, None] * frequency[None, :]
        cos_part = jnp.cos(angles)[:, None, :]
        sine_part = jnp.sin(angles)[:, None, :]
        low_half = values[..., start_col : start_col + half_width]
        high_half = values[..., start_col + half_width : start_col + width]
        outputs.append(low_half * cos_part - high_half * sine_part)
        outputs.append(low_half * sine_part + high_half * cos_part)
    return jnp.concatenate(outputs, axis=-1)


def frame_gates(levels, gate_w):
    level_frac = (levels.astype(jnp.float32) + 1.0) / LEVELS
    timestep = 1000.0 * flow_shift * level_frac / (1.0 + (flow_shift - 1.0) * level_frac)
    half_emb = gate_w.shape[0] // 2
    frequency = jnp.exp(-math.log(10000.0) * jnp.arange(half_emb, dtype=jnp.float32) / half_emb)
    angles = timestep[:, None] * frequency[None, :]
    embedding = jnp.concatenate([jnp.cos(angles), jnp.sin(angles)], axis=1)
    return jnp.dot(
        embedding,
        gate_w.astype(jnp.float32),
        precision=lax.Precision.HIGHEST,
        preferred_element_type=jnp.float32,
    )


def start_state(queries):
    row_count, head_count, head_dim = queries.shape
    return (
        jnp.full((head_count, row_count), -1e30, jnp.float32),
        jnp.zeros((head_count, row_count), jnp.float32),
        jnp.zeros((row_count, head_count, head_dim), jnp.float32),
    )


def absorb(state, queries, keys_block, values_block):
    row_max, row_sum, partial_value = state
    score_scale = 1.0 / math.sqrt(queries.shape[2])
    scores = (
        jnp.einsum("qhd,khd->hqk", queries, keys_block, preferred_element_type=jnp.float32)
        * score_scale
    )
    new_max = jnp.maximum(row_max, jnp.max(scores, axis=2))
    factor = jnp.exp(row_max - new_max)
    weights = jnp.exp(scores - new_max[:, :, None])
    row_sum = row_sum * factor + jnp.sum(weights, axis=2)
    partial_value = partial_value * jnp.transpose(factor)[:, :, None] + jnp.einsum(
        "hqk,khd->qhd",
        weights.astype(jnp.bfloat16),
        values_block,
        preferred_element_type=jnp.float32,
    )
    return (new_max, row_sum, partial_value)


def block_length(total_rows):
    for candidate in range(2048, 127, -128):
        return candidate
    return math.gcd(total_rows, 2048)


def absorb_all(state, queries, keys_block, values_block):
    total_rows, head_count, head_dim = keys_block.shape
    step_rows = block_length(total_rows)
    stacked = (
        keys_block.reshape(total_rows // step_rows, step_rows, head_count, head_dim),
        values_block.reshape(total_rows // step_rows, step_rows, head_count, head_dim),
    )

    def one_step(carry, block_pair):
        return (absorb(carry, queries, block_pair[0], block_pair[1]), None)

    state, unused = lax.scan(one_step, state, stacked)
    return state


def finish_rows(state):
    row_max, row_sum, partial_value = state
    row_count, head_count, head_dim = partial_value.shape
    return (
        (partial_value / jnp.transpose(row_sum)[:, :, None])
        .astype(jnp.bfloat16)
        .reshape(row_count, head_count * head_dim)
    )


def local(
    video_q,
    video_k,
    video_v,
    audio_q,
    audio_k,
    audio_v,
    video_x,
    audio_x,
    video_out_w,
    audio_out_w,
    video_gate_w,
    audio_gate_w,
    levels,
    video_pos,
    audio_pos,
):
    video_rows = video_q.shape[0]
    frame_count = video_pos.shape[0]
    device_rank = lax.axis_index(("vseq", "aseq"))
    frame_tokens = video_rows * lax.axis_size("vseq") * lax.axis_size("aseq") // frame_count
    token_index = device_rank * video_rows + jnp.arange(video_rows, dtype=jnp.int32)
    frame_of = token_index // frame_tokens
    within = token_index % frame_tokens
    frame_ids = jnp.arange(frame_count, dtype=jnp.int32)
    video_hot = frame_of[:, None] == frame_ids[None, :]
    place_t = jnp.sum(jnp.where(video_hot, video_pos[None, :], 0), axis=1)
    place_h = within // GRID_W
    place_w = within % GRID_W
    video_query = rotate(video_q.astype(jnp.float32), place_t, place_h, place_w).astype(
        jnp.bfloat16
    )
    video_key = rotate(video_k.astype(jnp.float32), place_t, place_h, place_w).astype(jnp.bfloat16)
    audio_frame = jnp.sum((video_pos[None, :] <= audio_pos[:, None]).astype(jnp.int32), axis=1) - 1
    audio_hot = audio_frame[:, None] == frame_ids[None, :]
    zero_place = jnp.zeros_like(audio_pos)
    audio_query = rotate(audio_q.astype(jnp.float32), audio_pos, zero_place, zero_place).astype(
        jnp.bfloat16
    )
    audio_key = rotate(audio_k.astype(jnp.float32), audio_pos, zero_place, zero_place).astype(
        jnp.bfloat16
    )
    video_query, video_key, video_value, audio_query, audio_key, audio_value = (
        lax.all_to_all(video_query, "aseq", split_axis=1, concat_axis=0, tiled=True),
        lax.all_to_all(video_key, "aseq", split_axis=1, concat_axis=0, tiled=True),
        lax.all_to_all(video_v, "aseq", split_axis=1, concat_axis=0, tiled=True),
        lax.all_to_all(audio_query, "aseq", split_axis=1, concat_axis=0, tiled=True),
        lax.all_to_all(audio_key, "aseq", split_axis=1, concat_axis=0, tiled=True),
        lax.all_to_all(audio_v, "aseq", split_axis=1, concat_axis=0, tiled=True),
    )
    opening = (start_state(video_query), start_state(audio_query))
    keys_video = lax.all_gather(video_key, "vseq", axis=0, tiled=True)
    values_video = lax.all_gather(video_value, "vseq", axis=0, tiled=True)
    keys_audio = lax.all_gather(audio_key, "vseq", axis=0, tiled=True)
    values_audio = lax.all_gather(audio_value, "vseq", axis=0, tiled=True)
    keys_joint = jnp.concatenate([keys_video, keys_audio], axis=0)
    values_joint = jnp.concatenate([values_video, values_audio], axis=0)
    video_state = absorb_all(opening[0], video_query, keys_joint, values_joint)
    audio_state = absorb_all(opening[1], audio_query, keys_joint, values_joint)
    video_state, audio_state = (video_state, audio_state)
    video_attn = finish_rows(video_state)
    audio_attn = finish_rows(audio_state)
    video_proj = lax.psum_scatter(
        jnp.dot(video_attn, video_out_w, preferred_element_type=jnp.float32).astype(jnp.bfloat16),
        "aseq",
        scatter_dimension=0,
        tiled=True,
    ).astype(jnp.float32)
    audio_proj = lax.psum_scatter(
        jnp.dot(audio_attn, audio_out_w, preferred_element_type=jnp.float32).astype(jnp.bfloat16),
        "aseq",
        scatter_dimension=0,
        tiled=True,
    ).astype(jnp.float32)
    video_gates = frame_gates(levels, video_gate_w)
    audio_gates = frame_gates(levels, audio_gate_w)
    video_row_gates = jnp.dot(
        video_hot.astype(jnp.float32),
        video_gates,
        precision=lax.Precision.HIGHEST,
        preferred_element_type=jnp.float32,
    )
    audio_row_gates = jnp.dot(
        audio_hot.astype(jnp.float32),
        audio_gates,
        precision=lax.Precision.HIGHEST,
        preferred_element_type=jnp.float32,
    )
    video_out = (video_x.astype(jnp.float32) + video_row_gates * video_proj).astype(jnp.bfloat16)
    audio_out = (audio_x.astype(jnp.float32) + audio_row_gates * audio_proj).astype(jnp.bfloat16)
    return (video_out, audio_out)


def solution(mesh):
    return jax.shard_map(
        local,
        mesh=mesh,
        in_specs=(
            P(("vseq", "aseq"), None, None),
            P(("vseq", "aseq"), None, None),
            P(("vseq", "aseq"), None, None),
            P(("vseq", "aseq"), None, None),
            P(("vseq", "aseq"), None, None),
            P(("vseq", "aseq"), None, None),
            P(("vseq", "aseq"), None),
            P(("vseq", "aseq"), None),
            P("aseq", None),
            P("aseq", None),
            P(),
            P(),
            P(),
            P(),
            P(("vseq", "aseq")),
        ),
        out_specs=(P(("vseq", "aseq"), None), P(("vseq", "aseq"), None)),
        check_vma=False,
    )
```

profile of v0, /device:TPU:38, one launch (start us, length us, event | category | flops | bytes accessed | tf_op | source)
XLA Modules:
  0.0 1008.9 jit_solution(17255857380148051269)
XLA Ops:
  10.9 15.5 %all_to_all.108 = bf16[8,24,128]{2,0,1:T(8,128)(2,1)S(1)} all-to-all(bf16[8,24,128]{2,0,1:T(8,128)(2,1)S(1)} %concatenate.28), channel_id=1, replica_groups=mesh['vseq'=32,'aseq'=8] {'aseq'}, dimensions={1} | all-to-all | bytes 98304 | tf_op jit(solution)/shard_map/all_to_all | solution.py:160
  32.5 2.6 concatenate.27
  35.0 17.9 %all_to_all.109 = bf16[48,24,128]{2,0,1:T(8,128)(2,1)S(1)} all-to-all(bf16[48,24,128]{2,0,1:T(8,128)(2,1)} %concatenate.27), channel_id=1, replica_groups=mesh['vseq'=32,'aseq'=8] {'aseq'}, dimensions={1} | all-to-all | bytes 589824 | tf_op jit(solution)/shard_map/all_to_all | solution.py:157
  54.6 10.4 %all_to_all.110 = bf16[8,24,128]{2,0,1:T(8,128)(2,1)S(1)} all-to-all(bf16[8,24,128]{2,0,1:T(8,128)(2,1)S(1)} %copy.64), channel_id=1, replica_groups=mesh['vseq'=32,'aseq'=8] {'aseq'}, dimensions={1} | all-to-all | bytes 98304 | tf_op jit(solution)/shard_map/all_to_all | solution.py:161
  66.7 17.7 %all_to_all.111 = bf16[48,24,128]{2,0,1:T(8,128)(2,1)S(1)} all-to-all(bf16[48,24,128]{2,0,1:T(8,128)(2,1)S(1)} %copy.62), channel_id=1, replica_groups=mesh['vseq'=32,'aseq'=8] {'aseq'}, dimensions={1} | all-to-all | bytes 589824 | tf_op jit(solution)/shard_map/all_to_all | solution.py:158
  86.8 4.0 all-to-all-start.5
  90.8 2.5 add_convert_fusion
  93.3 2.4 concatenate.30
  95.7 3.1 all-to-all-done.5
  98.8 4.0 all-to-all-start.2
  103.7 13.6 %all-to-all-done.2 = bf16[48,24,128]{2,0,1:T(8,128)(2,1)S(1)} async-done(((bf16[48,24,128]{2,0,1:T(8,128)(2,1)}), bf16[48,24,128]{2,0,1:T(8,128)(2,1)S(1)}, u32[]{:S(2)}, u32[]{:S(2)}) %all-to-all-start.2) | async-done | bytes 294944 | tf_op jit(solution)/shard_map/all_to_all | solution.py:156
  119.1 56.1 %all-gather.7.cloned.1.call-done = bf16[2048,3,128]{2,0,1:T(8,128)(2,1)} async-done(((bf16[64,3,128]{2,0,1:T(8,128)(2,1)}), bf16[2048,3,128]{2,0,1:T(8,128)(2,1)}) %all-gather.7.cloned.1.call-update) | async-done | bytes 1572880 | tf_op jit(solution)/shard_map/all_gather | solution.py:166
  175.2 222.6 %all-gather.5.cloned.1.call-done = bf16[12288,3,128]{2,0,1:T(8,128)(2,1)} async-done(((bf16[384,3,128]{2,0,1:T(8,128)(2,1)}), bf16[12288,3,128]{2,0,1:T(8,128)(2,1)}) %all-gather.5.cloned.1.call-update) | async-done | bytes 9437200 | tf_op jit(solution)/shard_map/all_gather | solution.py:164
  397.8 7.8 pad_maximum_fusion
  405.6 4.7 copy.66
  410.3 137.9 %all-gather.11.cloned.1.call-done = bf16[2048,3,128]{2,0,1:T(8,128)(2,1)} async-done(((bf16[64,3,128]{2,0,1:T(8,128)(2,1)}), bf16[2048,3,128]{2,0,1:T(8,128)(2,1)}) %all-gather.11.cloned.1.call-update) | async-done | bytes 1572880 | tf_op jit(solution)/shard_map/all_gather | solution.py:167
  548.1 220.6 %all-gather.9.cloned.1.call-done = bf16[12288,3,128]{2,0,1:T(8,128)(2,1)} async-done(((bf16[384,3,128]{2,0,1:T(8,128)(2,1)}), bf16[12288,3,128]{2,0,1:T(8,128)(2,1)}) %all-gather.9.cloned.1.call-update) | async-done | bytes 9437200 | tf_op jit(solution)/shard_map/all_gather | solution.py:165
  768.7 12.3 %pad_maximum_fusion.1 = bf16[14336,3,128]{2,0,1:T(8,128)(2,1)} fusion(bf16[2048,3,128]{2,0,1:T(8,128)(2,1)} %all-gather.11.cloned.1.call-done, bf16[12288,3,128]{2,0,1:T(8,128)(2,1)} %all-gather.9.cloned.1.call-done), kind=kLoop, calls=%fused_computation.46 | loop fusion | flops 22020096 | bytes 22020096 | tf_op jit(solution)/shard_map/concatenate | solution.py:169
  781.0 52.2 %while.31 = (s32[]{:T(128)}, f32[3,64]{1,0:T(4,128)S(1)}, f32[3,64]{1,0:T(4,128)S(1)}, f32[64,3,128]{2,0,1:T(8,128)S(1)}, bf16[7,2048,3,128]{3,1,2,0:T(8,128)(2,...) while((s32[]{:T(128)}, f32[3,64]{1,0:T(4,128)S(1)}, ...), condition=%wide.region_10.11_spmd.clone, body=%wide.region_7.10_spmd.clone.sunk | while | flops 203760768 | bytes 8122489 | solution.py:99
  781.0 3.3 fusion.100
  784.3 1.8 fusion.102
  786.1 2.4 fusion.104
  788.5 3.3 fusion.100
  791.7 1.8 fusion.102
  793.5 2.4 fusion.104
  795.9 3.3 fusion.100
  801.0 2.4 fusion.104
  803.4 3.3 fusion.100
  808.5 2.4 fusion.104
  810.8 3.3 fusion.100
  814.1 1.8 fusion.102
  815.9 2.4 fusion.104
  818.3 3.3 fusion.100
  823.4 2.4 fusion.104
  825.8 3.3 fusion.100
  830.8 2.4 fusion.104
  833.2 3.0 convolution_convert_fusion.1
  836.5 115.5 %while.30 = (s32[]{:T(128)}, f32[3,384]{1,0:T(4,128)S(1)}, f32[3,384]{1,0:T(4,128)S(1)}, f32[384,3,128]{0,2,1:T(8,128)S(1)}, bf16[7,2048,3,128]{3,1,2,0:T(8,128)...) while((s32[]{:T(128)}, f32[3,384]{1,0:T(4,128)S(1)}, ...), condition=%wide.region_4.5_spmd.clone, body=%wide.region_1.4_spmd.clone.sunk | while | flops 1227283200 | bytes 70754456 | solution.py:99
  836.5 6.4 bitcast_reduce_fusion.2
  843.0 5.4 fusion.94
  849.4 3.6 fusion.96
  853.0 6.4 bitcast_reduce_fusion.2
  859.5 5.4 fusion.94
  865.9 3.6 fusion.96
  869.6 6.4 bitcast_reduce_fusion.2
  876.0 5.4 fusion.94
  882.4 3.6 fusion.96
  886.1 6.4 bitcast_reduce_fusion.2
  892.5 5.4 fusion.94
  898.9 3.6 fusion.96
  902.5 6.4 bitcast_reduce_fusion.2
  909.0 5.4 fusion.94
  915.4 3.6 fusion.96
  919.0 6.4 bitcast_reduce_fusion.2
  925.5 5.4 fusion.94
  931.8 3.6 fusion.96
  935.5 6.4 bitcast_reduce_fusion.2
  942.0 5.4 fusion.94
  948.3 3.6 fusion.96
  952.1 2.9 convolution_convert_fusion
  955.3 2.1 fusion.55
  957.5 2.1 fusion.54
  961.3 38.6 %reduce-scatter.3.cloned.1.call-done = bf16[48,3072]{1,0:T(8,128)(2,1)} async-done(((bf16[384,3072]{1,0:T(8,128)(2,1)}), bf16[48,3072]{1,0:T(8,128)(2,1)}) %reduce-scatter.3.cloned.1.call-update) | async-done | bytes 294928 | tf_op jit(solution)/shard_map/reduce_scatter | solution.py:175
  999.9 2.1 fusion.48
  (135 shorter events, 34.5 us)
Async XLA Ops:
  7.2 944.9 %copy-start = (bf16[384,3072]{1,0:T(8,128)(2,1)S(1)}, bf16[384,3072]{1,0:T(8,128)(2,1)}, u32[]{:S(2)}) copy-start(bf16[384,3072]{1,0:T(8,128)(2,1)} %param.27) | copy-start | bytes 7077892
  7.2 168.0 %all-gather.7.cloned.1.call-start = ((), (), s32[]{:S(2)}) async-start(), calls=%async_computation.9 | async-start | bytes 1622016 | tf_op jit(solution)/shard_map/all_gather | solution.py:166
  27.0 370.8 %all-gather.5.cloned.1.call-start = ((), (), s32[]{:S(2)}) async-start(), calls=%async_computation.8 | async-start | bytes 9732096 | tf_op jit(solution)/shard_map/all_gather | solution.py:164
  28.3 4.2 copy-start.4
  28.3 4.1 copy-start.5
  28.3 4.1 copy-start.6
  28.3 4.1 copy-start.7
  53.7 494.4 %all-gather.11.cloned.1.call-start = ((), (), s32[]{:S(2)}) async-start(), calls=%async_computation.11 | async-start | bytes 1622016 | tf_op jit(solution)/shard_map/all_gather | solution.py:167
  65.7 703.0 %all-gather.9.cloned.1.call-start = ((), (), s32[]{:S(2)}) async-start(), calls=%async_computation.10 | async-start | bytes 9732096 | tf_op jit(solution)/shard_map/all_gather | solution.py:165
  86.8 12.0 %all-to-all-start.5 = ((bf16[8,24,128]{2,0,1:T(8,128)(2,1)}), bf16[8,24,128]{2,0,1:T(8,128)(2,1)}, u32[]{:S(2)}, u32[]{:S(2)}) async-start(bf16[8,24,128]{2,0,1:T(8,128)(2,1)} %concatenate.32), calls=%async_computation.6 | async-start | bytes 98304 | tf_op jit(solution)/shard_map/all_to_all | solution.py:159
  98.8 18.6 %all-to-all-start.2 = ((bf16[48,24,128]{2,0,1:T(8,128)(2,1)}), bf16[48,24,128]{2,0,1:T(8,128)(2,1)S(1)}, u32[]{:S(2)}, u32[]{:S(2)}) async-start(bf16[48,24,128]{2,0,1:T(8,128)(2,1)} %concatenate.30), calls=%async_computation.2 | async-start | bytes 589824 | tf_op jit(solution)/shard_map/all_to_all | solution.py:156
  102.8 856.8 %reduce-scatter.5.cloned.1.call-start = ((), (), s32[]{:S(2)}) async-start(), calls=%async_computation.13 | async-start | bytes 442368 | tf_op jit(solution)/shard_map/reduce_scatter | solution.py:181
  117.4 0.7 copy-start.2
  836.3 163.6 %reduce-scatter.3.cloned.1.call-start = ((), (), s32[]{:S(2)}) async-start(), calls=%async_computation.12 | async-start | bytes 2654208 | tf_op jit(solution)/shard_map/reduce_scatter | solution.py:175
  843.0 6.4 copy-start.1
  859.5 6.4 copy-start.1
  876.0 6.4 copy-start.1
  892.5 6.4 copy-start.1
  909.0 6.4 copy-start.1
  925.5 6.4 copy-start.1
  941.9 6.4 copy-start.1
  952.0 3.0 copy-start.9
  952.0 3.0 copy-start.10
  952.0 3.2 copy-start.11
  952.1 7.5 copy-start.8
  952.1 47.8 %copy-start.3 = (bf16[48,3072]{1,0:T(8,128)(2,1)S(1)}, bf16[48,3072]{1,0:T(8,128)(2,1)}, u32[]{:S(2)}) copy-start(bf16[48,3072]{1,0:T(8,128)(2,1)} %param.25) | copy-start | bytes 884740
Sparse Core Ops, SparseCore 0:
  27.1 148.0 all-gather.6
  177.5 220.1 all-gather.4
  399.6 148.5 all-gather.10
  549.8 218.8 all-gather.8
  836.4 37.5 reduce-scatter.4
  955.1 44.7 reduce-scatter.2
where the time goes:
time: 1010 us
  waiting for transfers between devices  693 us (69%)
  matrix products  124 us (12%)
  other arithmetic  82.3 us (8%)
  blocking collectives  61.5 us (6%)
  local copies, waits for them, and re-layouts  25.3 us (3%)
  between operations  14.4 us (1%)
    all_gather x1, waiting for transfers between devices, local(): keys_video = lax.all_gather(video_key, 'vseq', axis=0, tiled=True)  223 us
    all_gather x1, waiting for transfers between devices, local(): values_video = lax.all_gather(video_value, 'vseq', axis=0, tiled=True)  221 us
    all_gather x1, waiting for transfers between devices, local(): values_audio = lax.all_gather(audio_value, 'vseq', axis=0, tiled=True)  138 us
    dot_general x14, matrix products, absorb(): jnp.einsum('qhd,khd->hqk', queries, keys_block, preferred_element_type=jn...  67.9 us
    all_gather x1, waiting for transfers between devices, local(): keys_audio = lax.all_gather(audio_key, 'vseq', axis=0, tiled=True)  56.1 us
    reduce_sum x14, other arithmetic, absorb(): row_sum = row_sum * factor + jnp.sum(weights, axis=2)  50.1 us
    dot_general x14, matrix products, absorb(): jnp.einsum('hqk,khd->qhd', weights.astype(jnp.bfloat16), values_block, pr...  42.1 us
    reduce_scatter x1, waiting for transfers between devices, local(): lax.psum_scatter(jnp.dot(video_attn, video_out_w, preferred_element_type=...  38.6 us
  transfers between devices with their start and end apart: 8, of which 7 were waited for; matrix products, arithmetic and copies ran while one was open for 15% of the time, Pallas kernels for 0%

commit v1 on v0

v1 whole, which is shorter than its diff:
```python
import functools
import math

import jax
import jax.numpy as jnp
import numpy as np
from jax import lax
from jax.experimental import pallas as pl
from jax.experimental.pallas import tpu as pltpu
from jax.sharding import Mesh
from jax.sharding import PartitionSpec as P

GRID_W = 32
LEVELS = 1000
FLOW_SHIFT = 5.0
HEADS = 24
HD = 128
NX, NY, NZL, NZH, NC = 4, 4, 2, 4, 2
NZ = NZL * NZH
HPG = HEADS // NZ
TV_L = 48
TA_L = 8
T_L = TV_L + TA_L
ROWS = NZ * T_L
HALF = NZH * T_L
VHALF = NZH * TV_L
KEYS = NX * NC * ROWS
CHUNK = 512
STAT_ROWS = 64
O_ROWS = HPG * ROWS + STAT_ROWS
AXES = ("x", "y", "zl", "zh", "c")
VMEM = pl.BlockSpec(memory_space=pltpu.VMEM)
ANY = pl.BlockSpec(memory_space=pl.ANY)
NT = (((1,), (1,)), ((), ()))
TN = (((0,), (0,)), ((), ()))


def rope_lanes():
    sixth = HD // 6
    first = HD - 4 * sixth
    partner = np.zeros(HD, np.int32)
    sign = np.zeros(HD, np.float32)
    index = np.zeros(HD, np.float32)
    width_of = np.zeros(HD, np.float32)
    section = np.zeros(HD, np.int32)
    for number, (start, width) in enumerate(
        ((0, first), (first, 2 * sixth), (first + 2 * sixth, 2 * sixth))
    ):
        half = width // 2
        for k in range(half):
            low, high = start + k, start + half + k
            partner[low], partner[high] = high, low
            sign[low], sign[high] = -1.0, 1.0
            index[low] = index[high] = k
            width_of[low] = width_of[high] = width
            section[low] = section[high] = number
    return partner, sign, index, width_of, section


PARTNER, SIGN, INDEX, WIDTH_OF, SECTION = rope_lanes()


def group_of(z):
    return (z % NZH) * NZL + z // NZH


def prep_kernel(vq, vk, vv, aq, ak, av, swap, cos, sin, out):
    scale = math.log2(math.e) / math.sqrt(HD)
    cos_v, sin_v = cos[0:TV_L, :], sin[0:TV_L, :]
    cos_a, sin_a = cos[TV_L:T_L, :], sin[TV_L:T_L, :]
    tables = (
        (cos_v * scale, sin_v * scale, cos_a * scale, sin_a * scale),
        (cos_v, sin_v, cos_a, sin_a),
    )
    perm = swap[...]

    def turn(u, cos_part, sin_part):
        other = jnp.dot(u, perm, preferred_element_type=jnp.float32)
        return (u.astype(jnp.float32) * cos_part + other * sin_part).astype(jnp.bfloat16)

    for z in range(NZ):
        for h in range(HPG):
            lanes = slice((group_of(z) * HPG + h) * HD, (group_of(z) * HPG + h + 1) * HD)
            for t, (video, audio) in enumerate(((vq, aq), (vk, ak))):
                cv, sv, ca, sa = tables[t]
                out[z, t, h, 0:TV_L, :] = turn(video[:, lanes], cv, sv)
                out[z, t, h, TV_L:T_L, :] = turn(audio[:, lanes], ca, sa)
            out[z, 2, h, 0:TV_L, :] = vv[:, lanes]
            out[z, 2, h, TV_L:T_L, :] = av[:, lanes]


def arrange_kernel(got, q_out, kv_out):
    for z in range(NZ):
        zl, zh = z // NZH, z % NZH
        v_at = zl * HALF + zh * TV_L
        a_at = zl * HALF + VHALF + zh * TA_L
        for h in range(HPG):
            q_out[h, v_at : v_at + TV_L, :] = got[z, 0, h, 0:TV_L, :]
            q_out[h, a_at : a_at + TA_L, :] = got[z, 0, h, TV_L:T_L, :]
            for t in range(2):
                kv_out[t, h, v_at : v_at + TV_L, :] = got[z, 1 + t, h, 0:TV_L, :]
                kv_out[t, h, a_at : a_at + TA_L, :] = got[z, 1 + t, h, TV_L:T_L, :]


def attn_kernel(*refs):
    qs = refs[0:NY]
    kvs = refs[NY : NY + NX * NC]
    outs = refs[NY + NX * NC : NY + NX * NC + NY]
    qc, kc, vc, sc, mc, oc, lc, sems = refs[NY + NX * NC + NY :]
    n_kv = NX * NC
    copies = []
    for h in range(HPG):
        for a in range(n_kv):
            rows = pl.ds(a * ROWS, ROWS)
            copies.append(
                pltpu.make_async_copy(
                    kvs[a].at[0, h], kc.at[h, rows, :], sems.at[h * 2 * n_kv + 2 * a]
                )
            )
            copies.append(
                pltpu.make_async_copy(
                    kvs[a].at[1, h],
                    vc.at[h, rows, pl.ds(0, HD)],
                    sems.at[h * 2 * n_kv + 2 * a + 1],
                )
            )
    for copy in copies:
        copy.start()
    for h in range(HPG):
        vc[h, :, HD : 2 * HD] = jnp.ones((KEYS, HD), jnp.bfloat16)
        for s in range(NY):
            qc[h * NY + s] = qs[s][h]
    for copy in copies:
        copy.wait()
    n_chunks = KEYS // CHUNK

    def scores(tile, head, j, slot, top):
        s = lax.dot_general(
            qc[tile], kc[head, j * CHUNK : (j + 1) * CHUNK, :], NT,
            preferred_element_type=jnp.float32,
        )
        sc[slot, :, j * CHUNK : (j + 1) * CHUNK] = s
        part = s[:, 0:HD]
        for g in range(1, CHUNK // HD):
            part = jnp.maximum(part, s[:, g * HD : (g + 1) * HD])
        return part if top is None else jnp.maximum(top, part)

    def settle(top, slot):
        mc[slot] = jnp.broadcast_to(jnp.max(top, axis=1, keepdims=True), (ROWS, HD))

    def blend(head, j, slot, peak, total):
        s = sc[slot, :, j * CHUNK : (j + 1) * CHUNK]
        weights = jnp.concatenate(
            [
                jnp.exp2(s[:, g * HD : (g + 1) * HD] - peak).astype(jnp.bfloat16)
                for g in range(CHUNK // HD)
            ],
            axis=1,
        )
        new = jnp.dot(
            weights, vc[head, j * CHUNK : (j + 1) * CHUNK, :],
            preferred_element_type=jnp.float32,
        )
        return new if total is None else total + new

    def store(tile, peak, total):
        mass = total[:, HD : 2 * HD]
        oc[tile] = (total[:, 0:HD] / mass).astype(jnp.bfloat16)
        lc[tile] = peak + jnp.log2(mass)

    top = None
    for j in range(n_chunks):
        top = scores(0, 0, j, 0, top)
    settle(top, 0)

    def body(tile, carry):
        slot = lax.rem(tile, 2)
        head = tile // NY
        following = tile + 1
        next_head = following // NY
        peak = mc[slot]
        top, total = None, None
        for j in range(n_chunks):
            top = scores(following, next_head, j, 1 - slot, top)
            total = blend(head, j, slot, peak, total)
        settle(top, 1 - slot)
        store(tile, peak, total)
        return carry

    last = HPG * NY - 1
    lax.fori_loop(0, last, body, 0)
    peak = mc[last % 2]
    total = None
    for j in range(n_chunks):
        total = blend(HPG - 1, j, last % 2, peak, total)
    store(last, peak, total)

    lane = lax.broadcasted_iota(jnp.int32, (ROWS, HD), 1)
    eye = (
        lax.broadcasted_iota(jnp.int32, (16, HD), 0)
        == lax.broadcasted_iota(jnp.int32, (16, HD), 1)
    ).astype(jnp.bfloat16)
    for s in range(NY):
        stat = jnp.zeros((ROWS, HD), jnp.float32)
        for h in range(HPG):
            outs[s][h * ROWS : (h + 1) * ROWS, :] = oc[h * NY + s]
            level = lc[h * NY + s]
            for piece in range(3):
                short = level.astype(jnp.bfloat16).astype(jnp.float32)
                stat = jnp.where(lane == 3 * h + piece, short, stat)
                level = level - short
        turned = lax.dot_general(
            eye, stat.astype(jnp.bfloat16), NT, preferred_element_type=jnp.float32
        ).astype(jnp.bfloat16)
        turned = jnp.concatenate([turned, jnp.zeros((16, 4 * HD - ROWS), jnp.bfloat16)], axis=1)
        for g in range(4):
            at = HPG * ROWS + 16 * g
            outs[s][at : at + 16, :] = turned[:, g * HD : (g + 1) * HD]


def merge_kernel(zl_ref, o0, o1, o2, o3, keep, send, lm):
    eye = (
        lax.broadcasted_iota(jnp.int32, (16, HD), 0)
        == lax.broadcasted_iota(jnp.int32, (16, HD), 1)
    ).astype(jnp.bfloat16)
    parts = (o0, o1, o2, o3)
    for s, part in enumerate(parts):
        for g in range(4):
            at = HPG * ROWS + 16 * g
            lm[s, g * HD : (g + 1) * HD, :] = lax.dot_general(
                part[at : at + 16, :], eye, TN, preferred_element_type=jnp.float32
            )
    zl = zl_ref[0]
    for target, half in ((keep, zl), (send, 1 - zl)):
        off = pl.multiple_of(half * HALF, 32)
        stats = [lm[s, pl.ds(off, HALF), :] for s in range(NY)]
        for h in range(HPG):
            levels = [
                st[:, 3 * h : 3 * h + 1] + st[:, 3 * h + 1 : 3 * h + 2] + st[:, 3 * h + 2 : 3 * h + 3]
                for st in stats
            ]
            peak = functools.reduce(jnp.maximum, levels)
            shares = [jnp.exp2(level - peak) for level in levels]
            mass = functools.reduce(jnp.add, shares)
            total = None
            for s, part in enumerate(parts):
                rows = part[pl.ds(pl.multiple_of(h * ROWS + off, 32), HALF), :].astype(jnp.float32)
                term = rows * (shares[s] / mass)
                total = term if total is None else total + term
            target[:, h * HD : (h + 1) * HD] = total.astype(jnp.bfloat16)


def project_kernel(a_mine, a_other, wv_mine, wv_other, wa_mine, wa_other, out):
    def product(rows, mine, other):
        return (
            jnp.dot(a_mine[rows, :], mine[...], preferred_element_type=jnp.float32)
            + jnp.dot(a_other[rows, :], other[...], preferred_element_type=jnp.float32)
        ).astype(jnp.bfloat16)

    video = product(slice(0, VHALF), wv_mine, wv_other)
    audio = product(slice(VHALF, HALF), wa_mine, wa_other)
    for zh in range(NZH):
        out[zh, 0:TV_L, :] = video[zh * TV_L : (zh + 1) * TV_L, :]
        out[zh, TV_L:T_L, :] = audio[zh * TA_L : (zh + 1) * TA_L, :]


def params(mib):
    return pltpu.CompilerParams(vmem_limit_bytes=mib << 20)


def shift(array, axis, step, size):
    return lax.ppermute(array, axis, [(i, (i + step) % size) for i in range(size)])


def frame_gate(levels, frame, gate_w):
    level = lax.dynamic_slice(levels, (frame,), (1,)).astype(jnp.float32)
    level_frac = (level + 1.0) / LEVELS
    timestep = 1000.0 * FLOW_SHIFT * level_frac / (1.0 + (FLOW_SHIFT - 1.0) * level_frac)
    half_emb = gate_w.shape[0] // 2
    frequency = jnp.exp(-math.log(10000.0) * jnp.arange(half_emb, dtype=jnp.float32) / half_emb)
    angles = timestep[:, None] * frequency[None, :]
    embedding = jnp.concatenate([jnp.cos(angles), jnp.sin(angles)], axis=1)
    return jnp.dot(
        embedding,
        gate_w.astype(jnp.float32),
        precision=lax.Precision.HIGHEST,
        preferred_element_type=jnp.float32,
    )


def local(
    video_q, video_k, video_v, audio_q, audio_k, audio_v, video_x, audio_x,
    video_out_w, audio_out_w, video_gate_w, audio_gate_w, levels, video_pos, audio_pos,
):
    rank = lax.axis_index(AXES)
    width = HEADS * HD
    per_frame = NX * NY * NZ * NC // video_pos.shape[0]
    frame = rank // per_frame

    within = lax.rem(rank, per_frame) * TV_L + jnp.arange(TV_L, dtype=jnp.int32)
    place_t = jnp.concatenate(
        [jnp.broadcast_to(lax.dynamic_slice(video_pos, (frame,), (1,)), (TV_L,)), audio_pos]
    )
    zeros = jnp.zeros((TA_L,), jnp.int32)
    place_h = jnp.concatenate([within // GRID_W, zeros])
    place_w = jnp.concatenate([within % GRID_W, zeros])
    frequency = 10000.0 ** (-(jnp.asarray(INDEX) * 2.0) / jnp.asarray(WIDTH_OF))
    section = jnp.asarray(SECTION)[None, :]
    place = jnp.where(
        section == 0,
        place_t[:, None],
        jnp.where(section == 1, place_h[:, None], place_w[:, None]),
    ).astype(jnp.float32)
    angles = place * frequency[None, :]
    cos = jnp.cos(angles)
    sin = jnp.sin(angles) * jnp.asarray(SIGN)[None, :]
    swap = (jnp.arange(HD)[:, None] == jnp.asarray(PARTNER)[None, :]).astype(jnp.bfloat16)

    packed = pl.pallas_call(
        prep_kernel,
        out_shape=jax.ShapeDtypeStruct((NZ, 3, HPG, T_L, HD), jnp.bfloat16),
        in_specs=[VMEM] * 9,
        out_specs=VMEM,
        compiler_params=params(32),
    )(
        video_q.reshape(TV_L, width), video_k.reshape(TV_L, width), video_v.reshape(TV_L, width),
        audio_q.reshape(TA_L, width), audio_k.reshape(TA_L, width), audio_v.reshape(TA_L, width),
        swap, cos, sin,
    )
    got = lax.all_to_all(packed, ("zl", "zh"), split_axis=0, concat_axis=0, tiled=True)
    q_mine, kv_mine = pl.pallas_call(
        arrange_kernel,
        out_shape=(
            jax.ShapeDtypeStruct((HPG, ROWS, HD), jnp.bfloat16),
            jax.ShapeDtypeStruct((2, HPG, ROWS, HD), jnp.bfloat16),
        ),
        in_specs=[VMEM],
        out_specs=(VMEM, VMEM),
        compiler_params=params(32),
    )(got)

    kv_x = [kv_mine] + [shift(kv_mine, "x", s, NX) for s in (1, 3, 2)]
    kv_all = kv_x + [shift(kv, "c", 1, NC) for kv in kv_x]
    steps = (0, 1, 3, 2)
    q_all = [q_mine] + [shift(q_mine, "y", s, NY) for s in steps[1:]]
    wv_other = shift(video_out_w, "c", 1, NC)
    wa_other = shift(audio_out_w, "c", 1, NC)

    o_shape = jax.ShapeDtypeStruct((O_ROWS, HD), jnp.bfloat16)
    partial = pl.pallas_call(
        attn_kernel,
        out_shape=(o_shape,) * NY,
        in_specs=[VMEM] * NY + [ANY] * (NX * NC),
        out_specs=(VMEM,) * NY,
        scratch_shapes=[
            pltpu.VMEM((HPG * NY, ROWS, HD), jnp.bfloat16),
            pltpu.VMEM((HPG, KEYS, HD), jnp.bfloat16),
            pltpu.VMEM((HPG, KEYS, 2 * HD), jnp.bfloat16),
            pltpu.VMEM((2, ROWS, KEYS), jnp.float32),
            pltpu.VMEM((2, ROWS, HD), jnp.float32),
            pltpu.VMEM((HPG * NY, ROWS, HD), jnp.bfloat16),
            pltpu.VMEM((HPG * NY, ROWS, HD), jnp.float32),
            pltpu.SemaphoreType.DMA((HPG * 2 * NX * NC,)),
        ],
        compiler_params=params(52),
        cost_estimate=pl.CostEstimate(
            flops=4 * HPG * NY * ROWS * KEYS * HD,
            bytes_accessed=10 << 20,
            transcendentals=HPG * NY * ROWS * KEYS,
        ),
    )(*q_all, *kv_all)
    back = [partial[0]] + [
        shift(partial[i], "y", NY - steps[i], NY) for i in range(1, NY)
    ]
    zl = lax.axis_index("zl")
    c = lax.axis_index("c")
    a_shape = jax.ShapeDtypeStruct((HALF, HPG * HD), jnp.bfloat16)
    keep, send = pl.pallas_call(
        merge_kernel,
        out_shape=(a_shape, a_shape),
        in_specs=[pl.BlockSpec(memory_space=pltpu.SMEM)] + [VMEM] * NY,
        out_specs=(VMEM, VMEM),
        scratch_shapes=[pltpu.VMEM((NY, 4 * HD, HD), jnp.float32)],
        compiler_params=params(32),
    )(jnp.full((1,), zl, jnp.int32), *back)
    came = shift(send, "zl", 1, NZL)
    same = zl == c
    a_mine = jnp.where(same, keep, came)
    a_other = jnp.where(same, came, keep)

    cols = 768
    a_spec = pl.BlockSpec((HALF, HPG * HD), lambda i: (0, 0))
    w_spec = pl.BlockSpec((HPG * HD, cols), lambda i: (0, i))
    shares = pl.pallas_call(
        project_kernel,
        grid=(width // cols,),
        out_shape=jax.ShapeDtypeStruct((NZH, T_L, width), jnp.bfloat16),
        in_specs=[a_spec, a_spec, w_spec, w_spec, w_spec, w_spec],
        out_specs=pl.BlockSpec((NZH, T_L, cols), lambda i: (0, 0, i)),
        compiler_params=params(32),
    )(a_mine, a_other, video_out_w, wv_other, audio_out_w, wa_other)
    summed = lax.all_to_all(shares, "zh", split_axis=0, concat_axis=0, tiled=True)
    proj = jnp.sum(summed.astype(jnp.float32), axis=0)
    video_gate = frame_gate(levels, frame, video_gate_w)
    audio_gate = frame_gate(levels, frame, audio_gate_w)
    video_out = (video_x.astype(jnp.float32) + video_gate * proj[:TV_L]).astype(jnp.bfloat16)
    audio_out = (audio_x.astype(jnp.float32) + audio_gate * proj[TV_L:]).astype(jnp.bfloat16)
    return (video_out, audio_out)


def solution(mesh):
    fine = Mesh(mesh.devices.reshape(NX, NY, NZL, NZH, NC), AXES)
    tokens3 = P(AXES, None, None)
    tokens2 = P(AXES, None)
    weights = P(("zh", "c"), None)
    return jax.shard_map(
        local,
        mesh=fine,
        in_specs=(
            tokens3, tokens3, tokens3, tokens3, tokens3, tokens3,
            tokens2, tokens2, weights, weights, P(), P(), P(), P(), P(AXES),
        ),
        out_specs=(tokens2, tokens2),
        check_vma=False,
    )
```

time: 1010 us -> 209 us (0.21)
  waiting for transfers between devices: 693 us -> 78.2 us
  matrix products: 124 us -> 1.44 us
  other arithmetic: 82.3 us -> 2.62 us
  Pallas kernels: 0 us -> 62.4 us
  blocking collectives: 61.5 us -> 35.3 us
  local copies, waits for them, and re-layouts: 25.3 us -> 7.21 us
  between operations: 14.4 us -> 1.7 us
  starting transfers between devices: 8.42 us -> 19.5 us
    all_gather x4 -> x0, waiting for transfers between devices: 637 us -> none  [the longest x1 223 us: local(): keys_video = lax.all_gather(video_key, 'vseq', axis=0, tiled=True)]
    dot_general x34 -> x2, matrix products: 124 us -> 1.44 us  [frame_gate(): jnp.dot(embedding, gate_w.astype(jnp.float32), precision=lax.Precision.HI...]
    pallas_call x0 -> x5, Pallas kernels: none -> 62.4 us  [the longest x1 53 us: local(): pl.pallas_call(attn_kernel, out_shape=(o_shape,) * NY, in_specs=[VMEM] *...]
    reduce_sum x16 -> x1, other arithmetic: 51 us -> 0.22 us  [local(): proj = jnp.sum(summed.astype(jnp.float32), axis=0)]
    ppermute x0 -> x16, waiting for transfers between devices: none -> 48.2 us  [shift(): lax.ppermute(array, axis, [(i, (i + step) % size) for i in range(size)])]
    reduce_scatter x2 -> x0, waiting for transfers between devices: 38.6 us -> none  [the longest x1 38.6 us: local(): lax.psum_scatter(jnp.dot(video_attn, video_out_w, preferred_element_type=...]
    all_to_all x4 -> x1, blocking collectives: 61.5 us -> 35.3 us  [local(): lax.all_to_all(packed, ('zl', 'zh'), split_axis=0, concat_axis=0, tiled=T...]
    concatenate x2 -> x0, other arithmetic: 20.1 us -> none  [the longest x1 12.3 us: local(): values_joint = jnp.concatenate([values_video, values_audio], axis=0)]
  transfers between devices with their start and end apart: 8 -> 17, of which waited for: 7 -> 10; matrix products, arithmetic and copies ran while one was open for 15% -> 1% of each run, Pallas kernels for 0% -> 26%
where the time goes in v1:
time: 209 us; the launch traced here: 208 us
  waiting for transfers between devices  78.2 us (37%)
  Pallas kernels  62.4 us (30%)
  blocking collectives  35.3 us (17%)
  starting transfers between devices  19.5 us (9%)
  local copies, waits for them, and re-layouts  7.21 us (3%)
  other arithmetic  2.62 us (1%)
    pallas_call x1, Pallas kernels, local(): pl.pallas_call(attn_kernel, out_shape=(o_shape,) * NY, in_specs=[VMEM] *...  53 us
    ppermute x16, waiting for transfers between devices, shift(): lax.ppermute(array, axis, [(i, (i + step) % size) for i in range(size)])  48.2 us
    all_to_all x1, blocking collectives, local(): lax.all_to_all(packed, ('zl', 'zh'), split_axis=0, concat_axis=0, tiled=T...  35.3 us
    all_to_all x1, waiting for transfers between devices, local(): lax.all_to_all(shares, 'zh', split_axis=0, concat_axis=0, tiled=True)  30 us
    ppermute x16, starting transfers between devices, shift(): lax.ppermute(array, axis, [(i, (i + step) % size) for i in range(size)])  15.8 us
    pallas_call x1, Pallas kernels, local(): pl.pallas_call(project_kernel, grid=(width // cols,), out_shape=jax.Shape...  6.38 us
  transfers between devices with their start and end apart: 17, of which 10 were waited for; matrix products, arithmetic and copies ran while one was open for 1% of the time, Pallas kernels for 26%

profile of v1, /device:TPU:38, one launch (start us, length us, event | category | flops | bytes accessed | tf_op | source)
XLA Modules:
  0.0 208.3 jit_solution(3501122679434963510)
XLA Ops:
  0.6 0.0 copy-start
  0.6 0.0 copy-start.7
  0.7 0.0 copy-start.8
  0.7 0.0 copy-start.9
  0.7 0.0 copy-start.10
  0.7 0.0 copy-start.5
  0.7 0.0 copy-start.4
  0.8 1.1 copy.34
  1.9 0.8 copy.35
  2.7 0.7 fusion.4.swap
  3.4 1.2 dynamic_slice.8
  4.6 1.4 concatenate.14
  6.0 1.1 copy_bitcast_fusion
  7.2 0.0 copy-done.7
  7.2 0.2 sine_multiply_fusion
  7.4 1.0 shard_map.203
  8.4 35.3 %all_to_all.10.got = bf16[8,3,3,56,128]{4,3,2,1,0:T(8,128)(2,1)S(1)} all-to-all(bf16[8,3,3,56,128]{4,3,2,1,0:T(8,128)(2,1)S(1)} %shard_map.203), channel_id=1, replica_groups=mesh['x'=4,'y'=4,'zl'=2,'zh'=4,'c'=2] {'zl','zh'}, dimensions={0} | all-to-all | bytes 2064384 | tf_op jit(solution)/shard_map/all_to_all | solution.py:330
  43.7 0.1 shard_map.204
  43.7 1.7 collective-permute-start
  45.4 0.5 collective-permute-start.3
  45.9 1.5 collective-permute-start.4
  47.4 1.4 collective-permute-start.5
  48.8 1.7 collective-permute-start.1
  50.5 2.9 %collective-permute-done.refs_1_ = bf16[3,448,128]{2,1,0:T(8,128)(2,1)S(1)} collective-permute-done((bf16[3,448,128]{2,1,0:T(8,128)(2,1)S(1)}, bf16[3,448,128]{2,1,0:T(8,128)(2,1)S(1)}, u32[]{:S(2)}, u32[]{:S(2)}) %collective-permute-start) | collective-permute-done | bytes 344096 | tf_op jit(solution)/shard_map/ppermute | solution.py:272
  53.4 0.0 collective-permute-start.6
  53.4 2.7 %collective-permute-done.1.refs_2_ = bf16[3,448,128]{2,1,0:T(8,128)(2,1)S(1)} collective-permute-done((bf16[3,448,128]{2,1,0:T(8,128)(2,1)S(1)}, bf16[3,448,128]{2,1,0:T(8,128)(2,1)S(1)}, u32[]{:S(2)}, u32[]{:S(2)}) %collective-permute-start.1) | collective-permute-done | bytes 344096 | tf_op jit(solution)/shard_map/ppermute | solution.py:272
  56.1 2.9 %collective-permute-start.2 = (bf16[3,448,128]{2,1,0:T(8,128)(2,1)S(1)}, bf16[3,448,128]{2,1,0:T(8,128)(2,1)S(1)}, u32[]{:S(2)}, u32[]{:S(2)}) collective-permute-start(bf16[3,448,128]{2,1,0:T(8,128)(2,1)S(1)} %get-tuple-element.10.refs_0_), channel_id=1, source_target_pairs={{0,32},{16,48},{32,0},{48,16},{1,33},{17,49},{33,1},{49,17},{2,34}... | collective-permute-start | bytes 1032200 | tf_op jit(solution)/shard_map/ppermute | solution.py:272
  59.0 4.8 %collective-permute-done.3.refs_5_ = bf16[2,3,448,128]{3,2,1,0:T(8,128)(2,1)S(1)} collective-permute-done((bf16[2,3,448,128]{3,2,1,0:T(8,128)(2,1)S(1)}, bf16[2,3,448,128]{3,2,1,0:T(8,128)(2,1)S(1)}, u32[]{:S(2)}, u32[]{:S(2)}) %collective-permute-start.3) | collective-permute-done | bytes 688160 | tf_op jit(solution)/shard_map/ppermute | solution.py:272
  63.8 0.0 collective-permute-start.7
  63.8 13.2 %collective-permute-done.4.refs_6_ = bf16[2,3,448,128]{3,2,1,0:T(8,128)(2,1)S(1)} collective-permute-done((bf16[2,3,448,128]{3,2,1,0:T(8,128)(2,1)S(1)}, bf16[2,3,448,128]{3,2,1,0:T(8,128)(2,1)S(1)}, u32[]{:S(2)}, u32[]{:S(2)}) %collective-permute-start.4) | collective-permute-done | bytes 688160 | tf_op jit(solution)/shard_map/ppermute | solution.py:272
  77.0 0.0 collective-permute-start.8
  77.0 0.0 collective-permute-done.5.refs_7_
  77.0 0.5 collective-permute-start.9
  77.5 0.0 collective-permute-done.2.refs_3_
  77.5 0.1 collective-permute-start.14
  77.6 0.0 collective-permute-done.6.refs_8_
  77.6 0.4 collective-permute-start.15
  78.0 0.0 collective-permute-done.7.refs_9_
  78.0 1.1 collective-permute-done.8.refs_10_
  79.1 2.0 collective-permute-done.9.refs_11_
  81.1 0.9 copy-done.17
  82.0 53.0 %shard_map.205 = (bf16[1408,128]{1,0:T(8,128)(2,1)S(1)}, bf16[1408,128]{1,0:T(8,128)(2,1)}, bf16[1408,128]{1,0:T(8,128)(2,1)}, bf16[1408,128]{1,0:T(8,128)(2,1)}) custom-call(bf16[3,448,128]{2,1,0:T(8,128)(2,1)S(1)} %get-tuple-element.10.refs_0_, bf16[3,448,128]{2,1,0:T(8,128)(2,1)S(1)} %collective-permute-done.refs_1_, ...), custom_call_target="tpu_custom_call" | custom-call | flops 9865003008 | bytes 10485760 | tf_op jit(solution)/shard_map/pallas_call | solution.py:350
  135.0 1.9 collective-permute-start.10
  136.8 0.2 collective-permute-start.11
  137.1 2.9 %collective-permute-start.12 = (bf16[1408,128]{1,0:T(8,128)(2,1)}, bf16[1408,128]{1,0:T(8,128)(2,1)S(1)}, u32[]{:S(2)}, u32[]{:S(2)}) collective-permute-start(bf16[1408,128]{1,0:T(8,128)(2,1)} %get-tuple-element.15), channel_id=1, source_target_pairs={{0,32},{16,48},{32,0},{48,16},{1,33},{17,49},{33,1},{49,17},{2,34}... | collective-permute-start | bytes 1081352 | tf_op jit(solution)/shard_map/ppermute | solution.py:272
  140.0 12.9 %collective-permute-done.10.o1 = bf16[1408,128]{1,0:T(8,128)(2,1)S(1)} collective-permute-done((bf16[1408,128]{1,0:T(8,128)(2,1)}, bf16[1408,128]{1,0:T(8,128)(2,1)S(1)}, u32[]{:S(2)}, u32[]{:S(2)}) %collective-permute-start.10) | collective-permute-done | bytes 360480 | tf_op jit(solution)/shard_map/ppermute | solution.py:272
  152.9 3.3 %collective-permute-done.11.o2 = bf16[1408,128]{1,0:T(8,128)(2,1)S(1)} collective-permute-done((bf16[1408,128]{1,0:T(8,128)(2,1)}, bf16[1408,128]{1,0:T(8,128)(2,1)S(1)}, u32[]{:S(2)}, u32[]{:S(2)}) %collective-permute-start.11) | collective-permute-done | bytes 360480 | tf_op jit(solution)/shard_map/ppermute | solution.py:272
  156.2 0.0 collective-permute-done.12.o3
  156.2 2.1 shard_map.206
  158.2 0.1 collective-permute-start.13
  158.3 5.4 %collective-permute-done.13 = bf16[224,384]{1,0:T(8,128)(2,1)S(1)} collective-permute-done((bf16[224,384]{1,0:T(8,128)(2,1)S(1)}, bf16[224,384]{1,0:T(8,128)(2,1)S(1)}, u32[]{:S(2)}, u32[]{:S(2)}) %collective-permute-start.13) | collective-permute-done | bytes 172064 | tf_op jit(solution)/shard_map/ppermute | solution.py:272
  163.8 0.0 collective-permute-done.14.wv_other
  163.8 0.0 collective-permute-done.15.wa_other
  163.8 6.4 %shard_map.207 = bf16[4,56,3072]{2,1,0:T(8,128)(2,1)} custom-call(bf16[224,384]{1,0:T(8,128)(2,1)S(1)} %get-tuple-element.19.a_mine, bf16[224,384]{1,0:T(8,128)(2,1)S(1)} %get-tuple-element.18.a_other, bf16[384,3072]{1,0:T(8,128)(2,1)} %wv_mine.1, bf16[384,3072]{1,0:T(8,128)(2,1)} %collective-permute-done.14.wv_other, bf16[384,3072]{1,0:T(8,128)(2,1)} %wa_mine.1, ...), custom_call_target="tpu_custom_call" | custom-call | tf_op jit(solution)/shard_map/pallas_call | solution.py:394
  170.2 3.7 %all-to-all-start.1 = ((bf16[4,56,3072]{2,1,0:T(8,128)(2,1)}), bf16[4,56,3072]{2,1,0:T(8,128)(2,1)S(1)}, u32[]{:S(2)}, u32[]{:S(2)}) async-start(bf16[4,56,3072]{2,1,0:T(8,128)(2,1)} %shard_map.207), calls=%async_computation.1 | async-start | bytes 2752512 | tf_op jit(solution)/shard_map/all_to_all | solution.py:402
  173.9 0.6 dynamic_slice.7
  175.2 0.1 fusion.6
  175.2 0.7 fusion.8
  176.0 0.0 copy-start.3
  176.0 0.7 fusion.9
  176.7 30.0 %all-to-all-done.1 = bf16[4,56,3072]{2,1,0:T(8,128)(2,1)S(1)} async-done(((bf16[4,56,3072]{2,1,0:T(8,128)(2,1)}), bf16[4,56,3072]{2,1,0:T(8,128)(2,1)S(1)}, u32[]{:S(2)}, u32[]{:S(2)}) %all-to-all-start.1) | async-done | bytes 1376288 | tf_op jit(solution)/shard_map/all_to_all | solution.py:402
  206.6 0.2 convert_reduce_fusion
  206.9 0.6 fusion.3
  207.5 0.8 fusion.1
  (33 shorter events, 0.1 us)
Async XLA Ops:
  0.6 174.6 %copy-start = (bf16[256,3072]{1,0:T(8,128)(2,1)S(1)}, bf16[256,3072]{1,0:T(8,128)(2,1)}, u32[]{:S(2)}) copy-start(bf16[256,3072]{1,0:T(8,128)(2,1)} %param.31) | copy-start | bytes 4718596
  0.6 6.5 %copy-start.7 = (f32[128]{0:T(128)S(1)}, f32[128]{0:T(128)}, u32[]{:S(2)}) copy-start(f32[128]{0:T(128)} %constant.105.clone) | copy-start | bytes 1540
  0.7 6.5 %copy-start.8 = (pred[128]{0:T(512)(128)(4,1)S(1)}, pred[128]{0:T(512)(128)(4,1)}, u32[]{:S(2)}) copy-start(pred[128]{0:T(512)(128)(4,1)} %constant.123) | copy-start | bytes 388
  0.7 6.5 %copy-start.9 = (pred[128]{0:T(512)(128)(4,1)S(1)}, pred[128]{0:T(512)(128)(4,1)}, u32[]{:S(2)}) copy-start(pred[128]{0:T(512)(128)(4,1)} %constant.124) | copy-start | bytes 388
  0.7 6.5 %copy-start.10 = (f32[128]{0:T(128)S(1)}, f32[128]{0:T(128)}, u32[]{:S(2)}) copy-start(f32[128]{0:T(128)} %constant.128) | copy-start | bytes 1540
  0.7 6.4 %copy-start.5 = (bf16[8,24,128]{2,1,0:T(8,128)(2,1)S(1)}, bf16[8,24,128]{2,1,0:T(8,128)(2,1)}, u32[]{:S(2)}) copy-start(bf16[8,24,128]{2,1,0:T(8,128)(2,1)} %param.24) | copy-start | bytes 147460
  0.7 6.4 %copy-start.4 = (bf16[8,24,128]{2,1,0:T(8,128)(2,1)S(1)}, bf16[8,24,128]{2,1,0:T(8,128)(2,1)}, u32[]{:S(2)}) copy-start(bf16[8,24,128]{2,1,0:T(8,128)(2,1)} %param.25) | copy-start | bytes 147460
  43.7 37.3 %copy-start.1 = (bf16[2,3,448,128]{3,2,1,0:T(8,128)(2,1)}, bf16[2,3,448,128]{3,2,1,0:T(8,128)(2,1)S(1)}, u32[]{:S(2)}) copy-start(bf16[2,3,448,128]{3,2,1,0:T(8,128)(2,1)S(1)} %get-tuple-element.11.refs_4_) | copy-start | bytes 2064388
  43.7 9.7 %collective-permute-start = (bf16[3,448,128]{2,1,0:T(8,128)(2,1)S(1)}, bf16[3,448,128]{2,1,0:T(8,128)(2,1)S(1)}, u32[]{:S(2)}, u32[]{:S(2)}) collective-permute-start(bf16[3,448,128]{2,1,0:T(8,128)(2,1)S(1)} %get-tuple-element.10.refs_0_), channel_id=1, source_target_pairs={{0,16},{16,32},{32,48},{48,0},{1,17},{17,33},{33,49},{49,1},{2,18}... | collective-permute-start | bytes 1032200 | tf_op jit(solution)/shard_map/ppermute | solution.py:272
  45.4 18.4 %collective-permute-start.3 = (bf16[2,3,448,128]{3,2,1,0:T(8,128)(2,1)S(1)}, bf16[2,3,448,128]{3,2,1,0:T(8,128)(2,1)S(1)}, u32[]{:S(2)}, u32[]{:S(2)}) collective-permute-start(bf16[2,3,448,128]{3,2,1,0:T(8,128)(2,1)S(1)} %get-tuple-element.11.refs_4_), channel_id=1, source_target_pairs={{0,64},{64,128},{128,192},{192,0},{1,65},{65,129},{129,193},{193,1... | collective-permute-start | bytes 2064392 | tf_op jit(solution)/shard_map/ppermute | solution.py:272
  45.9 31.1 %collective-permute-start.4 = (bf16[2,3,448,128]{3,2,1,0:T(8,128)(2,1)S(1)}, bf16[2,3,448,128]{3,2,1,0:T(8,128)(2,1)S(1)}, u32[]{:S(2)}, u32[]{:S(2)}) collective-permute-start(bf16[2,3,448,128]{3,2,1,0:T(8,128)(2,1)S(1)} %get-tuple-element.11.refs_4_), channel_id=1, source_target_pairs={{0,192},{64,0},{128,64},{192,128},{1,193},{65,1},{129,65},{193,129... | collective-permute-start | bytes 2064392 | tf_op jit(solution)/shard_map/ppermute | solution.py:272
  47.4 29.5 %collective-permute-start.5 = (bf16[2,3,448,128]{3,2,1,0:T(8,128)(2,1)S(1)}, bf16[2,3,448,128]{3,2,1,0:T(8,128)(2,1)S(1)}, u32[]{:S(2)}, u32[]{:S(2)}) collective-permute-start(bf16[2,3,448,128]{3,2,1,0:T(8,128)(2,1)S(1)} %get-tuple-element.11.refs_4_), channel_id=1, source_target_pairs={{0,128},{64,192},{128,0},{192,64},{1,129},{65,193},{129,1},{193,65... | collective-permute-start | bytes 2064392 | tf_op jit(solution)/shard_map/ppermute | solution.py:272
  48.8 7.2 %collective-permute-start.1 = (bf16[3,448,128]{2,1,0:T(8,128)(2,1)S(1)}, bf16[3,448,128]{2,1,0:T(8,128)(2,1)S(1)}, u32[]{:S(2)}, u32[]{:S(2)}) collective-permute-start(bf16[3,448,128]{2,1,0:T(8,128)(2,1)S(1)} %get-tuple-element.10.refs_0_), channel_id=1, source_target_pairs={{0,48},{16,0},{32,16},{48,32},{1,49},{17,1},{33,17},{49,33},{2,50}... | collective-permute-start | bytes 1032200 | tf_op jit(solution)/shard_map/ppermute | solution.py:272
  53.4 24.2 %collective-permute-start.6 = (bf16[2,3,448,128]{3,2,1,0:T(8,128)(2,1)S(1)}, bf16[2,3,448,128]{3,2,1,0:T(8,128)(2,1)S(1)}, u32[]{:S(2)}, u32[]{:S(2)}) collective-permute-start(bf16[2,3,448,128]{3,2,1,0:T(8,128)(2,1)S(1)} %get-tuple-element.11.refs_4_), channel_id=1, source_target_pairs={{0,1},{1,0},{2,3},{3,2},{4,5},{5,4},{6,7},{7,6},{8,9},{9,8},{10,11... | collective-permute-start | bytes 2064392 | tf_op jit(solution)/shard_map/ppermute | solution.py:272
  56.1 21.4 %collective-permute-start.2 = (bf16[3,448,128]{2,1,0:T(8,128)(2,1)S(1)}, bf16[3,448,128]{2,1,0:T(8,128)(2,1)S(1)}, u32[]{:S(2)}, u32[]{:S(2)}) collective-permute-start(bf16[3,448,128]{2,1,0:T(8,128)(2,1)S(1)} %get-tuple-element.10.refs_0_), channel_id=1, source_target_pairs={{0,32},{16,48},{32,0},{48,16},{1,33},{17,49},{33,1},{49,17},{2,34}... | collective-permute-start | bytes 1032200 | tf_op jit(solution)/shard_map/ppermute | solution.py:272
  63.8 17.3 %copy-start.11 = (bf16[2,3,448,128]{3,2,1,0:T(8,128)(2,1)}, bf16[2,3,448,128]{3,2,1,0:T(8,128)(2,1)S(1)}, u32[]{:S(2)}) copy-start(bf16[2,3,448,128]{3,2,1,0:T(8,128)(2,1)S(1)} %collective-permute-done.3.refs_5_) | copy-start | bytes 2064388
  63.8 14.2 %collective-permute-start.7 = (bf16[2,3,448,128]{3,2,1,0:T(8,128)(2,1)S(1)}, bf16[2,3,448,128]{3,2,1,0:T(8,128)(2,1)S(1)}, u32[]{:S(2)}, u32[]{:S(2)}) collective-permute-start(bf16[2,3,448,128]{3,2,1,0:T(8,128)(2,1)S(1)} %collective-permute-done.3.refs_5_), channel_id=1, source_target_pairs={{0,1},{1,0},{2,3},{3,2},{4,5},{5,4},{6,7},{7,6},{8,9},{9,8},{10,11... | collective-permute-start | bytes 2064392 | tf_op jit(solution)/shard_map/ppermute | solution.py:272
  77.0 4.1 %copy-start.12 = (bf16[2,3,448,128]{3,2,1,0:T(8,128)(2,1)}, bf16[2,3,448,128]{3,2,1,0:T(8,128)(2,1)S(1)}, u32[]{:S(2)}) copy-start(bf16[2,3,448,128]{3,2,1,0:T(8,128)(2,1)S(1)} %collective-permute-done.4.refs_6_) | copy-start | bytes 2064388
  77.0 2.1 %collective-permute-start.8 = (bf16[2,3,448,128]{3,2,1,0:T(8,128)(2,1)S(1)}, bf16[2,3,448,128]{3,2,1,0:T(8,128)(2,1)S(1)}, u32[]{:S(2)}, u32[]{:S(2)}) collective-permute-start(bf16[2,3,448,128]{3,2,1,0:T(8,128)(2,1)S(1)} %collective-permute-done.4.refs_6_), channel_id=1, source_target_pairs={{0,1},{1,0},{2,3},{3,2},{4,5},{5,4},{6,7},{7,6},{8,9},{9,8},{10,11... | collective-permute-start | bytes 2064392 | tf_op jit(solution)/shard_map/ppermute | solution.py:272
  77.0 4.1 %copy-start.13 = (bf16[2,3,448,128]{3,2,1,0:T(8,128)(2,1)}, bf16[2,3,448,128]{3,2,1,0:T(8,128)(2,1)S(1)}, u32[]{:S(2)}) copy-start(bf16[2,3,448,128]{3,2,1,0:T(8,128)(2,1)S(1)} %collective-permute-done.5.refs_7_) | copy-start | bytes 2064388
  77.0 4.1 %collective-permute-start.9 = (bf16[2,3,448,128]{3,2,1,0:T(8,128)(2,1)S(1)}, bf16[2,3,448,128]{3,2,1,0:T(8,128)(2,1)S(1)}, u32[]{:S(2)}, u32[]{:S(2)}) collective-permute-start(bf16[2,3,448,128]{3,2,1,0:T(8,128)(2,1)S(1)} %collective-permute-done.5.refs_7_), channel_id=1, source_target_pairs={{0,1},{1,0},{2,3},{3,2},{4,5},{5,4},{6,7},{7,6},{8,9},{9,8},{10,11... | collective-permute-start | bytes 2064392 | tf_op jit(solution)/shard_map/ppermute | solution.py:272
  77.5 86.3 %collective-permute-start.14 = (bf16[384,3072]{1,0:T(8,128)(2,1)}, bf16[384,3072]{1,0:T(8,128)(2,1)}, u32[]{:S(2)}, u32[]{:S(2)}) collective-permute-start(bf16[384,3072]{1,0:T(8,128)(2,1)} %wv_mine.1), channel_id=1, source_target_pairs={{0,1},{1,0},{2,3},{3,2},{4,5},{5,4},{6,7},{7,6},{8,9},{9,8},{10,11... | collective-permute-start | bytes 7077896 | tf_op jit(solution)/shard_map/ppermute | solution.py:272
  77.6 3.5 %copy-start.14 = (bf16[2,3,448,128]{3,2,1,0:T(8,128)(2,1)}, bf16[2,3,448,128]{3,2,1,0:T(8,128)(2,1)S(1)}, u32[]{:S(2)}) copy-start(bf16[2,3,448,128]{3,2,1,0:T(8,128)(2,1)S(1)} %collective-permute-done.6.refs_8_) | copy-start | bytes 2064388
  77.6 86.2 %collective-permute-start.15 = (bf16[384,3072]{1,0:T(8,128)(2,1)}, bf16[384,3072]{1,0:T(8,128)(2,1)}, u32[]{:S(2)}, u32[]{:S(2)}) collective-permute-start(bf16[384,3072]{1,0:T(8,128)(2,1)} %wa_mine.1), channel_id=1, source_target_pairs={{0,1},{1,0},{2,3},{3,2},{4,5},{5,4},{6,7},{7,6},{8,9},{9,8},{10,11... | collective-permute-start | bytes 7077896 | tf_op jit(solution)/shard_map/ppermute | solution.py:272
  78.0 3.1 %copy-start.15 = (bf16[2,3,448,128]{3,2,1,0:T(8,128)(2,1)}, bf16[2,3,448,128]{3,2,1,0:T(8,128)(2,1)S(1)}, u32[]{:S(2)}) copy-start(bf16[2,3,448,128]{3,2,1,0:T(8,128)(2,1)S(1)} %collective-permute-done.7.refs_9_) | copy-start | bytes 2064388
  79.1 2.0 copy-start.16
  81.1 0.9 copy-start.17
  135.0 17.9 %collective-permute-start.10 = (bf16[1408,128]{1,0:T(8,128)(2,1)}, bf16[1408,128]{1,0:T(8,128)(2,1)S(1)}, u32[]{:S(2)}, u32[]{:S(2)}) collective-permute-start(bf16[1408,128]{1,0:T(8,128)(2,1)} %get-tuple-element.13), channel_id=1, source_target_pairs={{0,48},{16,0},{32,16},{48,32},{1,49},{17,1},{33,17},{49,33},{2,50}... | collective-permute-start | bytes 1081352 | tf_op jit(solution)/shard_map/ppermute | solution.py:272
  136.8 19.3 %collective-permute-start.11 = (bf16[1408,128]{1,0:T(8,128)(2,1)}, bf16[1408,128]{1,0:T(8,128)(2,1)S(1)}, u32[]{:S(2)}, u32[]{:S(2)}) collective-permute-start(bf16[1408,128]{1,0:T(8,128)(2,1)} %get-tuple-element.14), channel_id=1, source_target_pairs={{0,16},{16,32},{32,48},{48,0},{1,17},{17,33},{33,49},{49,1},{2,18}... | collective-permute-start | bytes 1081352 | tf_op jit(solution)/shard_map/ppermute | solution.py:272
  137.1 19.1 %collective-permute-start.12 = (bf16[1408,128]{1,0:T(8,128)(2,1)}, bf16[1408,128]{1,0:T(8,128)(2,1)S(1)}, u32[]{:S(2)}, u32[]{:S(2)}) collective-permute-start(bf16[1408,128]{1,0:T(8,128)(2,1)} %get-tuple-element.15), channel_id=1, source_target_pairs={{0,32},{16,48},{32,0},{48,16},{1,33},{17,49},{33,1},{49,17},{2,34}... | collective-permute-start | bytes 1081352 | tf_op jit(solution)/shard_map/ppermute | solution.py:272
  158.2 5.5 %collective-permute-start.13 = (bf16[224,384]{1,0:T(8,128)(2,1)S(1)}, bf16[224,384]{1,0:T(8,128)(2,1)S(1)}, u32[]{:S(2)}, u32[]{:S(2)}) collective-permute-start(bf16[224,384]{1,0:T(8,128)(2,1)S(1)} %get-tuple-element.17), channel_id=1, source_target_pairs={{0,8},{8,0},{1,9},{9,1},{2,10},{10,2},{3,11},{11,3},{4,12},{12,4},... | collective-permute-start | bytes 516104 | tf_op jit(solution)/shard_map/ppermute | solution.py:272
  170.2 3.7 %copy-start.18 = (s32[8]{0:T(128)S(1)}, s32[8]{0:T(128)}, u32[]{:S(2)}) copy-start(s32[8]{0:T(128)} %param.32) | copy-start | bytes 100
  170.2 36.5 %all-to-all-start.1 = ((bf16[4,56,3072]{2,1,0:T(8,128)(2,1)}), bf16[4,56,3072]{2,1,0:T(8,128)(2,1)S(1)}, u32[]{:S(2)}, u32[]{:S(2)}) async-start(bf16[4,56,3072]{2,1,0:T(8,128)(2,1)} %shard_map.207), calls=%async_computation.1 | async-start | bytes 2752512 | tf_op jit(solution)/shard_map/all_to_all | solution.py:402
  173.9 2.1 copy-start.2
  176.0 30.9 %copy-start.6 = (bf16[8,3072]{1,0:T(8,128)(2,1)S(1)}, bf16[8,3072]{1,0:T(8,128)(2,1)}, u32[]{:S(2)}) copy-start(bf16[8,3072]{1,0:T(8,128)(2,1)} %param.27) | copy-start | bytes 147460
  176.0 31.6 %copy-start.3 = (bf16[48,3072]{1,0:T(8,128)(2,1)S(1)}, bf16[48,3072]{1,0:T(8,128)(2,1)}, u32[]{:S(2)}) copy-start(bf16[48,3072]{1,0:T(8,128)(2,1)} %param.26) | copy-start | bytes 884740

commit v2 on v1

v2 whole, which is shorter than its diff:
```python
import functools
import math

import jax
import jax.numpy as jnp
import numpy as np
from jax import lax
from jax.experimental import pallas as pl
from jax.experimental.pallas import tpu as pltpu
from jax.sharding import Mesh
from jax.sharding import PartitionSpec as P

GRID_W = 32
GRID_SHIFT = 5
LEVELS = 1000
FLOW_SHIFT = 5.0
HEADS = 24
HD = 128
NX, NY, NZL, NZH, NC = 4, 4, 2, 4, 2
NZ = NZL * NZH
HPG = HEADS // NZ
TV_L = 48
TA_L = 8
T_L = TV_L + TA_L
ROWS = NZ * T_L
HALF = NZH * T_L
VHALF = NZH * TV_L
CHUNK = 512
STAT = 16
AXES = ("x", "y", "zl", "zh", "c")
VMEM = pl.BlockSpec(memory_space=pltpu.VMEM)
SMEM = pl.BlockSpec(memory_space=pltpu.SMEM)
ANY = pl.BlockSpec(memory_space=pl.ANY)
NT = (((1,), (1,)), ((), ()))
TN = (((0,), (0,)), ((), ()))


def rope_lanes():
    sixth = HD // 6
    first = HD - 4 * sixth
    partner = np.zeros(HD, np.int32)
    sign = np.zeros(HD, np.float32)
    index = np.zeros(HD, np.float32)
    width_of = np.zeros(HD, np.float32)
    section = np.zeros(HD, np.int32)
    for number, (start, width) in enumerate(
        ((0, first), (first, 2 * sixth), (first + 2 * sixth, 2 * sixth))
    ):
        half = width // 2
        for k in range(half):
            low, high = start + k, start + half + k
            partner[low], partner[high] = high, low
            sign[low], sign[high] = -1.0, 1.0
            index[low] = index[high] = k
            width_of[low] = width_of[high] = width
            section[low] = section[high] = number
    return partner, sign, index, width_of, section


PARTNER, SIGN, INDEX, WIDTH_OF, SECTION = rope_lanes()


def group_of(z):
    return (z % NZH) * NZL + z // NZH


def prep_kernel(vpos, apos, vq, vk, vv, aq, ak, av, swap, tables, out):
    scale = math.log2(math.e) / math.sqrt(HD)
    rank = jnp.int32(0)
    for name, size in zip(AXES, (NX, NY, NZL, NZH, NC)):
        rank = rank * size + lax.axis_index(name)
    per_frame = NX * NY * NZ * NC // vpos.shape[0]
    frame = lax.div(rank, jnp.int32(per_frame))
    start = lax.rem(rank, jnp.int32(per_frame)) * TV_L
    row_v = lax.broadcasted_iota(jnp.int32, (TV_L, HD), 0)
    row_a = lax.broadcasted_iota(jnp.int32, (TA_L, HD), 0)
    within = start + row_v
    high = within >> GRID_SHIFT
    wide = within & (GRID_W - 1)
    section_v = jnp.broadcast_to(tables[2:3, :], (TV_L, HD))
    place_v = jnp.where(
        section_v == 0.0,
        vpos[frame].astype(jnp.float32),
        jnp.where(section_v == 1.0, high.astype(jnp.float32), wide.astype(jnp.float32)),
    )
    place_a = jnp.zeros((TA_L, HD), jnp.int32)
    for i in range(TA_L):
        place_a = jnp.where(row_a == i, apos[i], place_a)
    section_a = jnp.broadcast_to(tables[2:3, :], (TA_L, HD))
    place_a = jnp.where(section_a == 0.0, place_a.astype(jnp.float32), 0.0)
    perm = swap[...]

    def turn(ref, place, gain):
        n, heads, hd = ref.shape
        angles = place * tables[0:1, :]
        cos = jnp.cos(angles) * gain
        sin = jnp.sin(angles) * tables[1:2, :] * gain
        u = jnp.swapaxes(ref[...], 0, 1)
        other = jnp.dot(
            u.reshape(heads * n, hd), perm, preferred_element_type=jnp.float32
        ).reshape(heads, n, hd)
        return (u.astype(jnp.float32) * cos[None] + other * sin[None]).astype(jnp.bfloat16)

    for t, (video, audio, gain) in enumerate(((vq, aq, scale), (vk, ak, 1.0), (vv, av, None))):
        if gain is None:
            video, audio = jnp.swapaxes(video[...], 0, 1), jnp.swapaxes(audio[...], 0, 1)
        else:
            video, audio = turn(video, place_v, gain), turn(audio, place_a, gain)
        for z in range(NZ):
            for h in range(HPG):
                out[z, t, h, 0:TV_L, :] = video[group_of(z) * HPG + h]
                out[z, t, h, TV_L:T_L, :] = audio[group_of(z) * HPG + h]


def arrange_kernel(got, q_out, kv_out):
    for z in range(NZ):
        zl, zh = z // NZH, z % NZH
        v_at = zl * HALF + zh * TV_L
        a_at = zl * HALF + VHALF + zh * TA_L
        for h in range(HPG):
            q_out[h, v_at : v_at + TV_L, :] = got[z, 0, h, 0:TV_L, :]
            q_out[h, a_at : a_at + TA_L, :] = got[z, 0, h, TV_L:T_L, :]
            for t in range(2):
                kv_out[t, h, v_at : v_at + TV_L, :] = got[z, 1 + t, h, 0:TV_L, :]
                kv_out[t, h, a_at : a_at + TA_L, :] = got[z, 1 + t, h, TV_L:T_L, :]


def eye_tile():
    return (
        lax.broadcasted_iota(jnp.int32, (STAT, HD), 0)
        == lax.broadcasted_iota(jnp.int32, (STAT, HD), 1)
    ).astype(jnp.bfloat16)


def stat_tile(level):
    lane = lax.broadcasted_iota(jnp.int32, (ROWS, HD), 1)
    row = lax.broadcasted_iota(jnp.int32, (ROWS, HD), 0)
    stat = jnp.zeros((ROWS, HD), jnp.float32)
    for piece in range(3):
        short = level.astype(jnp.bfloat16).astype(jnp.float32)
        stat = jnp.where(lane == 3 * (row >> 7) + piece, short, stat)
        level = level - short
    stat = stat.astype(jnp.bfloat16)
    tile = None
    for at in range(0, ROWS, HD):
        size = min(HD, ROWS - at)
        part = lax.dot_general(
            eye_tile(), stat[at : at + size, :], NT, preferred_element_type=jnp.float32
        )
        if size < HD:
            part = jnp.concatenate([part, jnp.zeros((STAT, HD - size), jnp.float32)], axis=1)
        tile = part if tile is None else tile + part
    return tile.astype(jnp.bfloat16)


def stat_level(tile):
    flat = lax.dot_general(tile, eye_tile(), TN, preferred_element_type=jnp.float32)
    pieces = []
    for g in range(-(-ROWS // HD)):
        size = min(HD, ROWS - g * HD)
        pieces.append(
            flat[0:size, 3 * g : 3 * g + 1]
            + flat[0:size, 3 * g + 1 : 3 * g + 2]
            + flat[0:size, 3 * g + 2 : 3 * g + 3]
        )
    return jnp.broadcast_to(jnp.concatenate(pieces, axis=0), (ROWS, HD))


def attn_kernel(n_q, n_pair, n_split, with_prev, final, *refs):
    refs = list(refs)

    def take(count):
        taken, refs[:count] = refs[:count], []
        return taken

    qs, pairs, splits = take(n_q), take(n_pair), take(2 * n_split)
    prev = take(2) if with_prev else None
    outs = take(n_q if final else 2)
    qc, kc, vc, oc, lc, sems = refs
    n_kv = n_pair + n_split
    rows, keys = n_q * ROWS, n_kv * ROWS
    copies = []
    for h in range(HPG):
        for a in range(n_kv):
            if a < n_pair:
                k_from, v_from = pairs[a].at[0, h], pairs[a].at[1, h]
            else:
                k_from, v_from = (ref.at[h] for ref in splits[2 * (a - n_pair) :][:2])
            place = pl.ds(a * ROWS, ROWS)
            at = 2 * (h * n_kv + a)
            copies.append(pltpu.make_async_copy(k_from, kc.at[h, place, :], sems.at[at]))
            copies.append(
                pltpu.make_async_copy(v_from, vc.at[h, place, pl.ds(0, HD)], sems.at[at + 1])
            )
    for copy in copies:
        copy.start()
    for h in range(HPG):
        vc[h, :, HD : 2 * HD] = jnp.ones((keys, HD), jnp.bfloat16)
        for s in range(n_q):
            qc[h, s * ROWS : (s + 1) * ROWS, :] = qs[s][h]
    for copy in copies:
        copy.wait()
    cuts = [(at, min(CHUNK, keys - at)) for at in range(0, keys, CHUNK)]

    def body(head, carry):
        queries = qc[head]

        def scores(cut):
            at, size = cut
            return lax.dot_general(
                queries, kc[head, at : at + size, :], NT, preferred_element_type=jnp.float32
            )

        s = scores(cuts[0])
        peak = total = None
        for number, (at, size) in enumerate(cuts):
            coming = scores(cuts[number + 1]) if number + 1 < len(cuts) else None
            slabs = [s[:, g : g + HD] for g in range(0, size, HD)]
            top = jnp.max(functools.reduce(jnp.maximum, slabs), axis=1, keepdims=True)
            top = jnp.broadcast_to(top, (rows, HD))
            if peak is not None:
                top = jnp.maximum(peak, top)
            weights = jnp.concatenate(
                [jnp.exp2(slab - top).astype(jnp.bfloat16) for slab in slabs], axis=1
            )
            new = jnp.dot(
                weights, vc[head, at : at + size, :], preferred_element_type=jnp.float32
            )
            if total is None:
                total = new
            else:
                factor = jnp.exp2(peak - top)
                total = total * jnp.concatenate([factor, factor], axis=1) + new
            peak, s = top, coming
        mass = total[:, HD : 2 * HD]
        oc[head] = total[:, 0:HD] / mass
        lc[head] = peak + jnp.log2(mass)
        return carry

    lax.fori_loop(0, HPG, body, 0)
    for h in range(HPG):
        for s in range(n_q):
            span = slice(s * ROWS, (s + 1) * ROWS)
            value, level = oc[h, span, :], lc[h, span, :]
            if with_prev:
                at = (h * n_q + s) * STAT
                before = stat_level(prev[1][at : at + STAT, :])
                top = jnp.maximum(level, before)
                here, there = jnp.exp2(level - top), jnp.exp2(before - top)
                both = here + there
                value = (value * here + prev[0][h, span, :] * there) / both
                level = top + jnp.log2(both)
            if final:
                at = h * (ROWS + STAT)
                outs[s][at : at + ROWS, :] = value.astype(jnp.bfloat16)
                outs[s][at + ROWS : at + ROWS + STAT, :] = stat_tile(level)
            else:
                outs[0][h, span, :] = value
                outs[1][(h * n_q + s) * STAT : (h * n_q + s + 1) * STAT, :] = stat_tile(level)


def attention(queries, pairs, splits, prev, final):
    n_q, n_pair, n_split = len(queries), len(pairs), len(splits) // 2
    rows, keys = n_q * ROWS, (n_pair + n_split) * ROWS
    if final:
        shapes = (jax.ShapeDtypeStruct((HPG * (ROWS + STAT), HD), jnp.bfloat16),) * n_q
    else:
        shapes = (
            jax.ShapeDtypeStruct((HPG, rows, HD), jnp.float32),
            jax.ShapeDtypeStruct((HPG * n_q * STAT, HD), jnp.bfloat16),
        )
    prev = () if prev is None else tuple(prev)
    return pl.pallas_call(
        functools.partial(attn_kernel, n_q, n_pair, n_split, bool(prev), final),
        out_shape=shapes,
        in_specs=[VMEM] * n_q + [ANY] * (n_pair + 2 * n_split) + [VMEM] * len(prev),
        out_specs=(VMEM,) * len(shapes),
        scratch_shapes=[
            pltpu.VMEM((HPG, rows, HD), jnp.bfloat16),
            pltpu.VMEM((HPG, keys, HD), jnp.bfloat16),
            pltpu.VMEM((HPG, keys, 2 * HD), jnp.bfloat16),
            pltpu.VMEM((HPG, rows, HD), jnp.float32),
            pltpu.VMEM((HPG, rows, HD), jnp.float32),
            pltpu.SemaphoreType.DMA((2 * HPG * (n_pair + n_split),)),
        ],
        compiler_params=params(52),
        cost_estimate=pl.CostEstimate(
            flops=16 * HPG * rows * keys * HD,
            bytes_accessed=8 << 20,
            transcendentals=HPG * rows * keys,
        ),
    )(*queries, *pairs, *splits, *prev)


def merge_kernel(zl_ref, o0, o1, o2, o3, keep, send, merged):
    parts = (o0, o1, o2, o3)
    for h in range(HPG):
        at = h * (ROWS + STAT)
        levels = [stat_level(part[at + ROWS : at + ROWS + STAT, :]) for part in parts]
        peak = functools.reduce(jnp.maximum, levels)
        shares = [jnp.exp2(level - peak) for level in levels]
        mass = functools.reduce(jnp.add, shares)
        total = functools.reduce(
            jnp.add,
            [part[at : at + ROWS, :].astype(jnp.float32) * w for part, w in zip(parts, shares)],
        )
        merged[:, h * HD : (h + 1) * HD] = (total / mass).astype(jnp.bfloat16)
    zl = zl_ref[0]
    keep[...] = merged[pl.ds(pl.multiple_of(zl * HALF, 32), HALF), :]
    send[...] = merged[pl.ds(pl.multiple_of((1 - zl) * HALF, 32), HALF), :]


def project_kernel(a_mine, a_other, wv_mine, wv_other, wa_mine, wa_other, out):
    def product(rows, mine, other):
        return (
            jnp.dot(a_mine[rows, :], mine[...], preferred_element_type=jnp.float32)
            + jnp.dot(a_other[rows, :], other[...], preferred_element_type=jnp.float32)
        ).astype(jnp.bfloat16)

    video = product(slice(0, VHALF), wv_mine, wv_other)
    audio = product(slice(VHALF, HALF), wa_mine, wa_other)
    for zh in range(NZH):
        out[zh, 0:TV_L, :] = video[zh * TV_L : (zh + 1) * TV_L, :]
        out[zh, TV_L:T_L, :] = audio[zh * TA_L : (zh + 1) * TA_L, :]


def params(mib):
    return pltpu.CompilerParams(vmem_limit_bytes=mib << 20)


def shift(array, axis, step, size):
    return lax.ppermute(array, axis, [(i, (i + step) % size) for i in range(size)])


def frame_gate(levels, frame, gate_w):
    level = lax.dynamic_slice(levels, (frame,), (1,)).astype(jnp.float32)
    level_frac = (level + 1.0) / LEVELS
    timestep = 1000.0 * FLOW_SHIFT * level_frac / (1.0 + (FLOW_SHIFT - 1.0) * level_frac)
    half_emb = gate_w.shape[0] // 2
    frequency = jnp.exp(-math.log(10000.0) * jnp.arange(half_emb, dtype=jnp.float32) / half_emb)
    angles = timestep[:, None] * frequency[None, :]
    embedding = jnp.concatenate([jnp.cos(angles), jnp.sin(angles)], axis=1)
    return jnp.dot(
        embedding,
        gate_w.astype(jnp.float32),
        precision=lax.Precision.HIGHEST,
        preferred_element_type=jnp.float32,
    )


def local(
    video_q, video_k, video_v, audio_q, audio_k, audio_v, video_x, audio_x,
    video_out_w, audio_out_w, video_gate_w, audio_gate_w, levels, video_pos, audio_pos,
):
    width = HEADS * HD
    rank = lax.axis_index(AXES)
    frame = rank // (NX * NY * NZ * NC // video_pos.shape[0])
    frequency = 10000.0 ** (-(INDEX * np.float32(2.0)) / WIDTH_OF)
    tables = jnp.asarray(
        np.concatenate(
            [
                np.stack([frequency, SIGN, SECTION]).astype(np.float32),
                np.zeros((5, HD), np.float32),
            ]
        )
    )
    swap = jnp.asarray(np.arange(HD)[:, None] == PARTNER[None, :], jnp.bfloat16)
    packed = pl.pallas_call(
        prep_kernel,
        out_shape=jax.ShapeDtypeStruct((NZ, 3, HPG, T_L, HD), jnp.bfloat16),
        in_specs=[SMEM] * 2 + [VMEM] * 8,
        out_specs=VMEM,
        compiler_params=params(32),
    )(
        video_pos, audio_pos, video_q, video_k, video_v, audio_q, audio_k, audio_v, swap, tables
    )
    got = lax.all_to_all(packed, ("zl", "zh"), split_axis=0, concat_axis=0, tiled=True)
    q_mine, kv_mine = pl.pallas_call(
        arrange_kernel,
        out_shape=(
            jax.ShapeDtypeStruct((HPG, ROWS, HD), jnp.bfloat16),
            jax.ShapeDtypeStruct((2, HPG, ROWS, HD), jnp.bfloat16),
        ),
        in_specs=[VMEM],
        out_specs=(VMEM, VMEM),
        compiler_params=params(32),
    )(got)

    kv_left = shift(kv_mine, "x", 1, NX)
    kv_right = shift(kv_mine, "x", NX - 1, NX)
    steps = (1, NY - 1, 2)
    q_far = [shift(q_mine, "y", step, NY) for step in steps]
    pairs = [kv_mine, kv_left, kv_right]
    k_far = shift(kv_left[0], "x", 1, NX)
    v_far = shift(kv_right[1], "x", NX - 1, NX)
    pairs = pairs + [shift(kv, "c", 1, NC) for kv in pairs]
    wv_other = shift(video_out_w, "c", 1, NC)
    wa_other = shift(audio_out_w, "c", 1, NC)

    first = attention(q_far, pairs, [], None, False)
    k_far, v_far, *first = lax.optimization_barrier((k_far, v_far, *first))
    splits = [k_far, v_far, shift(k_far, "c", 1, NC), shift(v_far, "c", 1, NC)]
    partial = attention(q_far, [], splits, first, True)
    back = [shift(part, "y", NY - step, NY) for part, step in zip(partial, steps)]
    own = attention([q_mine], pairs, splits, None, True)
    back = list(own) + back
    zl = lax.axis_index("zl")
    c = lax.axis_index("c")
    a_shape = jax.ShapeDtypeStruct((HALF, HPG * HD), jnp.bfloat16)
    keep, send = pl.pallas_call(
        merge_kernel,
        out_shape=(a_shape, a_shape),
        in_specs=[SMEM] + [VMEM] * NY,
        out_specs=(VMEM, VMEM),
        scratch_shapes=[pltpu.VMEM((ROWS, HPG * HD), jnp.bfloat16)],
        compiler_params=params(32),
    )(jnp.full((1,), zl, jnp.int32), *back)
    came = shift(send, "zl", 1, NZL)
    same = zl == c
    a_mine = jnp.where(same, keep, came)
    a_other = jnp.where(same, came, keep)

    cols = 768
    a_spec = pl.BlockSpec((HALF, HPG * HD), lambda i: (0, 0))
    w_spec = pl.BlockSpec((HPG * HD, cols), lambda i: (0, i))
    shares = pl.pallas_call(
        project_kernel,
        grid=(width // cols,),
        out_shape=jax.ShapeDtypeStruct((NZH, T_L, width), jnp.bfloat16),
        in_specs=[a_spec, a_spec, w_spec, w_spec, w_spec, w_spec],
        out_specs=pl.BlockSpec((NZH, T_L, cols), lambda i: (0, 0, i)),
        compiler_params=params(32),
    )(a_mine, a_other, video_out_w, wv_other, audio_out_w, wa_other)
    summed = lax.all_to_all(shares, "zh", split_axis=0, concat_axis=0, tiled=True)
    proj = jnp.sum(summed.astype(jnp.float32), axis=0)
    video_gate = frame_gate(levels, frame, video_gate_w)
    audio_gate = frame_gate(levels, frame, audio_gate_w)
    video_out = (video_x.astype(jnp.float32) + video_gate * proj[:TV_L]).astype(jnp.bfloat16)
    audio_out = (audio_x.astype(jnp.float32) + audio_gate * proj[TV_L:]).astype(jnp.bfloat16)
    return (video_out, audio_out)


def solution(mesh):
    fine = Mesh(mesh.devices.reshape(NX, NY, NZL, NZH, NC), AXES)
    tokens3 = P(AXES, None, None)
    tokens2 = P(AXES, None)
    weights = P(("zh", "c"), None)
    return jax.shard_map(
        local,
        mesh=fine,
        in_specs=(
            tokens3, tokens3, tokens3, tokens3, tokens3, tokens3,
            tokens2, tokens2, weights, weights, P(), P(), P(), P(), P(AXES),
        ),
        out_specs=(tokens2, tokens2),
        check_vma=False,
    )
```

time: 209 us -> 201 us (0.962)
  Pallas kernels: 62.4 us -> 52.9 us
  local copies, waits for them, and re-layouts: 7.21 us -> 14.7 us
  waiting for transfers between devices: 78.2 us -> 71.3 us
    unnamed x40 -> x56, local copies, waits for them, and re-layouts: 2.86 us -> 14 us
    pallas_call x2 -> x4, Pallas kernels: 55 us -> 45.3 us  [the longest x3 41.8 us: attention(): pl.pallas_call(functools.partial(attn_kernel, n_q, n_pair, n_split, bool(...]
    ppermute x16 -> x18, waiting for transfers between devices: 48.2 us -> 41.3 us  [shift(): lax.ppermute(array, axis, [(i, (i + step) % size) for i in range(size)])]
    ppermute x16 -> x18, starting transfers between devices: 15.8 us -> 15.9 us  [shift(): lax.ppermute(array, axis, [(i, (i + step) % size) for i in range(size)])]
  transfers between devices with their start and end apart: 17 -> 19, of which waited for: 10 -> 9; matrix products, arithmetic and copies ran while one was open for 1% -> 1% of each run, Pallas kernels for 26% -> 23%
where the time goes in v2:
time: 201 us; the launch traced here: 199 us
  waiting for transfers between devices  71.3 us (35%)
  Pallas kernels  52.9 us (26%)
  blocking collectives  35.3 us (18%)
  starting transfers between devices  19.6 us (10%)
  local copies, waits for them, and re-layouts  14.7 us (7%)
    pallas_call x3, Pallas kernels, attention(): pl.pallas_call(functools.partial(attn_kernel, n_q, n_pair, n_split, bool(...  41.8 us
    ppermute x18, waiting for transfers between devices, shift(): lax.ppermute(array, axis, [(i, (i + step) % size) for i in range(size)])  41.3 us
    all_to_all x1, blocking collectives, local(): lax.all_to_all(packed, ('zl', 'zh'), split_axis=0, concat_axis=0, tiled=T...  35.3 us
    all_to_all x1, waiting for transfers between devices, local(): lax.all_to_all(shares, 'zh', split_axis=0, concat_axis=0, tiled=True)  30.1 us
    ppermute x18, starting transfers between devices, shift(): lax.ppermute(array, axis, [(i, (i + step) % size) for i in range(size)])  15.9 us
    unnamed x56, local copies, waits for them, and re-layouts  14 us
    pallas_call x1, Pallas kernels, local(): pl.pallas_call(project_kernel, grid=(width // cols,), out_shape=jax.Shape...  6.35 us
  transfers between devices with their start and end apart: 19, of which 9 were waited for; matrix products, arithmetic and copies ran while one was open for 1% of the time, Pallas kernels for 23%

profile of v2, /device:TPU:38, one launch (start us, length us, event | category | flops | bytes accessed | tf_op | source)
XLA Modules:
  0.0 198.5 jit_solution(114388180046377871)
XLA Ops:
  0.6 0.0 copy-start
  0.7 1.1 copy-done.2
  1.7 1.0 copy-done.3
  2.7 1.0 copy-done.4
  3.7 0.8 copy-done.5
  4.5 0.8 copy-done.6
  5.3 0.8 copy-done.7
  6.1 0.8 copy-done.8
  6.8 0.7 copy-done.9
  7.5 0.7 copy-done.10
  8.2 0.7 copy-done.11
  8.8 1.2 shard_map.176
  10.0 35.3 %all_to_all.10.got = bf16[8,3,3,56,128]{4,3,2,1,0:T(8,128)(2,1)S(1)} all-to-all(bf16[8,3,3,56,128]{4,3,2,1,0:T(8,128)(2,1)S(1)} %shard_map.176), channel_id=1, replica_groups=mesh['x'=4,'y'=4,'zl'=2,'zh'=4,'c'=2] {'zl','zh'}, dimensions={0} | all-to-all | bytes 2064384 | tf_op jit(solution)/shard_map/all_to_all | solution.py:377
  45.3 0.1 shard_map.177
  45.4 0.6 collective-permute-start
  45.9 1.5 collective-permute-start.1
  47.5 1.6 collective-permute-start.7
  49.1 0.0 collective-permute-start.2
  49.1 12.1 %collective-permute-done.refs_4_.refs_2_ = bf16[2,3,448,128]{3,2,1,0:T(8,128)(2,1)S(1)} collective-permute-done((bf16[2,3,448,128]{3,2,1,0:T(8,128)(2,1)S(1)}, bf16[2,3,448,128]{3,2,1,0:T(8,128)(2,1)S(1)}, u32[]{:S(2)}, u32[]{:S(2)}) %collective-permute-start) | collective-permute-done | bytes 688160 | tf_op jit(solution)/shard_map/ppermute | solution.py:332
  61.1 1.4 collective-permute-done.1.refs_5_.refs_3_
  62.6 0.0 collective-permute-start.4
  62.6 3.0 %collective-permute-start.8 = (bf16[3,448,128]{2,1,0:T(8,128)(2,1)S(1)}, bf16[3,448,128]{2,1,0:T(8,128)(2,1)S(1)}, u32[]{:S(2)}, u32[]{:S(2)}) collective-permute-start(bf16[3,448,128]{2,1,0:T(8,128)(2,1)S(1)} %get-tuple-element.15.refs_0_), channel_id=1, source_target_pairs={{0,48},{16,0},{32,16},{48,32},{1,49},{17,1},{33,17},{49,33},{2,50}... | collective-permute-start | bytes 1032200 | tf_op jit(solution)/shard_map/ppermute | solution.py:332
  65.6 0.6 collective-permute-start.9
  66.3 14.7 %collective-permute-done.8.refs_1_ = bf16[3,448,128]{2,1,0:T(8,128)(2,1)S(1)} collective-permute-done((bf16[3,448,128]{2,1,0:T(8,128)(2,1)S(1)}, bf16[3,448,128]{2,1,0:T(8,128)(2,1)S(1)}, u32[]{:S(2)}, u32[]{:S(2)}) %collective-permute-start.8) | collective-permute-done | bytes 344096 | tf_op jit(solution)/shard_map/ppermute | solution.py:332
  80.9 0.4 collective-permute-start.5
  81.3 1.6 collective-permute-start.6
  83.0 0.0 collective-permute-done.2.refs_6_.refs_4_
  83.0 0.0 collective-permute-done.3.refs_7_.refs_5_
  83.0 0.8 copy-done.24
  83.8 0.3 copy-done.25
  84.1 0.9 copy-done.26
  84.9 18.2 %shard_map.178 = (f32[3,1344,128]{2,1,0:T(8,128)}, bf16[144,128]{1,0:T(8,128)(2,1)S(1)}) custom-call(bf16[3,448,128]{2,1,0:T(8,128)(2,1)S(1)} %collective-permute-done.7.refs_0_, bf16[3,448,128]{2,1,0:T(8,128)(2,1)S(1)} %collective-permute-done.8.refs_1_, bf16[3,448,128]{2,1,0:T(8,128)(2,1)S(1)} %collective-permute-done.9.refs_2_, ...), custom_call_target="tpu_custom_call" | custom-call | flops 22196256768 | bytes 8388608 | tf_op jit(solution)/shard_map/pallas_call | solution.py:273
  103.2 0.1 collective-permute-start.10
  103.3 0.5 collective-permute-start.11
  103.8 0.1 collective-permute-start.16
  103.9 0.4 collective-permute-start.17
  104.3 0.6 collective-permute-done.10.refs_9_.refs_5_
  105.0 0.8 collective-permute-done.11.refs_10_.refs_6_
  105.8 1.0 copy-done.14
  106.8 1.0 copy-done.16
  107.8 13.2 %shard_map.180 = (bf16[1392,128]{1,0:T(8,128)(2,1)}, bf16[1392,128]{1,0:T(8,128)(2,1)}, bf16[1392,128]{1,0:T(8,128)(2,1)}) custom-call(bf16[3,448,128]{2,1,0:T(8,128)(2,1)S(1)} %collective-permute-done.7.refs_0_, bf16[3,448,128]{2,1,0:T(8,128)(2,1)S(1)} %copy-done.14, bf16[3,448,128]{2,1,0:T(8,128)(2,1)S(1)} %copy-done.16, ...), custom_call_target="tpu_custom_call" | custom-call | flops 7398752256 | bytes 8388608 | tf_op jit(solution)/shard_map/pallas_call | solution.py:273
  121.0 3.8 %collective-permute-start.12 = (bf16[1392,128]{1,0:T(8,128)(2,1)}, bf16[1392,128]{1,0:T(8,128)(2,1)S(1)}, u32[]{:S(2)}, u32[]{:S(2)}) collective-permute-start(bf16[1392,128]{1,0:T(8,128)(2,1)} %get-tuple-element.23), channel_id=1, source_target_pairs={{0,48},{16,0},{32,16},{48,32},{1,49},{17,1},{33,17},{49,33},{2,50}... | collective-permute-start | bytes 1069064 | tf_op jit(solution)/shard_map/ppermute | solution.py:332
  124.8 0.0 collective-permute-start.13
  124.8 1.6 collective-permute-start.14
  126.3 1.0 copy-done.18
  127.3 10.4 %shard_map.179.o0 = bf16[1392,128]{1,0:T(8,128)(2,1)} custom-call(bf16[3,448,128]{2,1,0:T(8,128)(2,1)S(1)} %get-tuple-element.15.refs_0_, bf16[2,3,448,128]{3,2,1,0:T(8,128)(2,1)} %copy-done.12, bf16[2,3,448,128]{3,2,1,0:T(8,128)(2,1)} %copy-done.21, bf16[2,3,448,128]{3,2,1,0:T(8,128)(2,1)} %copy-done.22, bf16[2,3,448,128]{3,2,1,0:T(8,128)(2,1)} %copy-done.24, ...), custom_call_target="tpu_custom_call" | custom-call | flops 9865003008 | bytes 8388608 | tf_op jit(solution)/shard_map/pallas_call | solution.py:273
  137.7 2.9 %collective-permute-done.12.o1 = bf16[1392,128]{1,0:T(8,128)(2,1)S(1)} collective-permute-done((bf16[1392,128]{1,0:T(8,128)(2,1)}, bf16[1392,128]{1,0:T(8,128)(2,1)S(1)}, u32[]{:S(2)}, u32[]{:S(2)}) %collective-permute-start.12) | collective-permute-done | bytes 356384 | tf_op jit(solution)/shard_map/ppermute | solution.py:332
  140.6 3.3 %collective-permute-done.13.o2 = bf16[1392,128]{1,0:T(8,128)(2,1)S(1)} collective-permute-done((bf16[1392,128]{1,0:T(8,128)(2,1)}, bf16[1392,128]{1,0:T(8,128)(2,1)S(1)}, u32[]{:S(2)}, u32[]{:S(2)}) %collective-permute-start.13) | collective-permute-done | bytes 356384 | tf_op jit(solution)/shard_map/ppermute | solution.py:332
  143.9 1.0 copy-done.1
  144.9 3.4 %shard_map.181 = (bf16[224,384]{1,0:T(8,128)(2,1)S(1)}, bf16[224,384]{1,0:T(8,128)(2,1)S(1)}) custom-call(s32[1]{0:T(128)} %bitcast.4.zl_ref, bf16[1392,128]{1,0:T(8,128)(2,1)S(1)} %copy-done.1, bf16[1392,128]{1,0:T(8,128)(2,1)S(1)} %collective-permute-done.12.o1, bf16[1392,128]{1,0:T(8,128)(2,1)S(1)} %collective-permute-done.13.o2, ...), custom_call_target="tpu_custom_call" | custom-call | tf_op jit(solution)/shard_map/pallas_call | solution.py:410
  148.3 0.1 collective-permute-start.15
  148.4 5.4 %collective-permute-done.15 = bf16[224,384]{1,0:T(8,128)(2,1)S(1)} collective-permute-done((bf16[224,384]{1,0:T(8,128)(2,1)S(1)}, bf16[224,384]{1,0:T(8,128)(2,1)S(1)}, u32[]{:S(2)}, u32[]{:S(2)}) %collective-permute-start.15) | collective-permute-done | bytes 172064 | tf_op jit(solution)/shard_map/ppermute | solution.py:332
  153.9 0.0 collective-permute-done.16.wv_other
  153.9 6.4 %shard_map.182 = bf16[4,56,3072]{2,1,0:T(8,128)(2,1)} custom-call(bf16[224,384]{1,0:T(8,128)(2,1)S(1)} %get-tuple-element.29.a_mine, bf16[224,384]{1,0:T(8,128)(2,1)S(1)} %get-tuple-element.28.a_other, bf16[384,3072]{1,0:T(8,128)(2,1)} %wv_mine.1, bf16[384,3072]{1,0:T(8,128)(2,1)} %collective-permute-done.16.wv_other, bf16[384,3072]{1,0:T(8,128)(2,1)} %wa_mine.1, ...), custom_call_target="tpu_custom_call" | custom-call | tf_op jit(solution)/shard_map/pallas_call | solution.py:426
  160.3 3.7 %all-to-all-start.1 = ((bf16[4,56,3072]{2,1,0:T(8,128)(2,1)}), bf16[4,56,3072]{2,1,0:T(8,128)(2,1)S(1)}, u32[]{:S(2)}, u32[]{:S(2)}) async-start(bf16[4,56,3072]{2,1,0:T(8,128)(2,1)} %shard_map.182), calls=%async_computation.1 | async-start | bytes 2752512 | tf_op jit(solution)/shard_map/all_to_all | solution.py:434
  164.0 0.0 copy-start.19
  164.0 0.6 dynamic_slice.4
  165.3 0.1 fusion.4
  165.3 0.7 fusion.7
  166.1 0.7 fusion.6
  166.8 30.1 %all-to-all-done.1 = bf16[4,56,3072]{2,1,0:T(8,128)(2,1)S(1)} async-done(((bf16[4,56,3072]{2,1,0:T(8,128)(2,1)}), bf16[4,56,3072]{2,1,0:T(8,128)(2,1)S(1)}, u32[]{:S(2)}, u32[]{:S(2)}) %all-to-all-start.1) | async-done | bytes 1376288 | tf_op jit(solution)/shard_map/all_to_all | solution.py:434
  196.9 0.2 convert_reduce_fusion
  197.1 0.8 fusion.1
  197.9 0.6 fusion.3
  (48 shorter events, 0.2 us)
Async XLA Ops:
  0.6 164.7 %copy-start = (bf16[256,3072]{1,0:T(8,128)(2,1)S(1)}, bf16[256,3072]{1,0:T(8,128)(2,1)}, u32[]{:S(2)}) copy-start(bf16[256,3072]{1,0:T(8,128)(2,1)} %param.27) | copy-start | bytes 4718596
  0.6 1.1 copy-start.2
  1.7 1.0 copy-start.3
  2.7 1.0 copy-start.4
  3.7 0.8 copy-start.5
  4.5 0.8 copy-start.6
  5.3 0.8 copy-start.7
  6.0 0.8 copy-start.8
  6.8 0.7 copy-start.9
  7.5 0.7 copy-start.10
  8.2 0.7 copy-start.11
  45.4 57.8 %copy-start.12 = (bf16[2,3,448,128]{3,2,1,0:T(8,128)(2,1)}, bf16[2,3,448,128]{3,2,1,0:T(8,128)(2,1)S(1)}, u32[]{:S(2)}) copy-start(bf16[2,3,448,128]{3,2,1,0:T(8,128)(2,1)S(1)} %get-tuple-element.16.refs_3_.refs_1_) | copy-start | bytes 2064388
  45.4 15.8 %collective-permute-start = (bf16[2,3,448,128]{3,2,1,0:T(8,128)(2,1)S(1)}, bf16[2,3,448,128]{3,2,1,0:T(8,128)(2,1)S(1)}, u32[]{:S(2)}, u32[]{:S(2)}) collective-permute-start(bf16[2,3,448,128]{3,2,1,0:T(8,128)(2,1)S(1)} %get-tuple-element.16.refs_3_.refs_1_), channel_id=1, source_target_pairs={{0,64},{64,128},{128,192},{192,0},{1,65},{65,129},{129,193},{193,1... | collective-permute-start | bytes 2064392 | tf_op jit(solution)/shard_map/ppermute | solution.py:332
  45.9 16.6 %collective-permute-start.1 = (bf16[2,3,448,128]{3,2,1,0:T(8,128)(2,1)S(1)}, bf16[2,3,448,128]{3,2,1,0:T(8,128)(2,1)S(1)}, u32[]{:S(2)}, u32[]{:S(2)}) collective-permute-start(bf16[2,3,448,128]{3,2,1,0:T(8,128)(2,1)S(1)} %get-tuple-element.16.refs_3_.refs_1_), channel_id=1, source_target_pairs={{0,192},{64,0},{128,64},{192,128},{1,193},{65,1},{129,65},{193,129... | collective-permute-start | bytes 2064392 | tf_op jit(solution)/shard_map/ppermute | solution.py:332
  47.5 18.1 %collective-permute-start.7 = (bf16[3,448,128]{2,1,0:T(8,128)(2,1)S(1)}, bf16[3,448,128]{2,1,0:T(8,128)(2,1)S(1)}, u32[]{:S(2)}, u32[]{:S(2)}) collective-permute-start(bf16[3,448,128]{2,1,0:T(8,128)(2,1)S(1)} %get-tuple-element.15.refs_0_), channel_id=1, source_target_pairs={{0,16},{16,32},{32,48},{48,0},{1,17},{17,33},{33,49},{49,1},{2,18}... | collective-permute-start | bytes 1032200 | tf_op jit(solution)/shard_map/ppermute | solution.py:332
  49.1 33.9 %collective-permute-start.2 = (bf16[2,3,448,128]{3,2,1,0:T(8,128)(2,1)S(1)}, bf16[2,3,448,128]{3,2,1,0:T(8,128)(2,1)S(1)}, u32[]{:S(2)}, u32[]{:S(2)}) collective-permute-start(bf16[2,3,448,128]{3,2,1,0:T(8,128)(2,1)S(1)} %get-tuple-element.16.refs_3_.refs_1_), channel_id=1, source_target_pairs={{0,1},{1,0},{2,3},{3,2},{4,5},{5,4},{6,7},{7,6},{8,9},{9,8},{10,11... | collective-permute-start | bytes 2064392 | tf_op jit(solution)/shard_map/ppermute | solution.py:332
  61.1 21.9 %copy-start.21 = (bf16[2,3,448,128]{3,2,1,0:T(8,128)(2,1)}, bf16[2,3,448,128]{3,2,1,0:T(8,128)(2,1)S(1)}, u32[]{:S(2)}) copy-start(bf16[2,3,448,128]{3,2,1,0:T(8,128)(2,1)S(1)} %collective-permute-done.refs_4_.refs_2_) | copy-start | bytes 2064388
  61.1 21.8 %collective-permute-start.3 = (bf16[2,3,448,128]{3,2,1,0:T(8,128)(2,1)S(1)}, bf16[2,3,448,128]{3,2,1,0:T(8,128)(2,1)S(1)}, u32[]{:S(2)}, u32[]{:S(2)}) collective-permute-start(bf16[2,3,448,128]{3,2,1,0:T(8,128)(2,1)S(1)} %collective-permute-done.refs_4_.refs_2_), channel_id=1, source_target_pairs={{0,1},{1,0},{2,3},{3,2},{4,5},{5,4},{6,7},{7,6},{8,9},{9,8},{10,11... | collective-permute-start | bytes 2064392 | tf_op jit(solution)/shard_map/ppermute | solution.py:332
  62.6 20.5 %copy-start.22 = (bf16[2,3,448,128]{3,2,1,0:T(8,128)(2,1)}, bf16[2,3,448,128]{3,2,1,0:T(8,128)(2,1)S(1)}, u32[]{:S(2)}) copy-start(bf16[2,3,448,128]{3,2,1,0:T(8,128)(2,1)S(1)} %collective-permute-done.1.refs_5_.refs_3_) | copy-start | bytes 2064388
  62.6 20.4 %collective-permute-start.4 = (bf16[2,3,448,128]{3,2,1,0:T(8,128)(2,1)S(1)}, bf16[2,3,448,128]{3,2,1,0:T(8,128)(2,1)S(1)}, u32[]{:S(2)}, u32[]{:S(2)}) collective-permute-start(bf16[2,3,448,128]{3,2,1,0:T(8,128)(2,1)S(1)} %collective-permute-done.1.refs_5_.refs_3_), channel_id=1, source_target_pairs={{0,1},{1,0},{2,3},{3,2},{4,5},{5,4},{6,7},{7,6},{8,9},{9,8},{10,11... | collective-permute-start | bytes 2064392 | tf_op jit(solution)/shard_map/ppermute | solution.py:332
  62.6 18.4 %collective-permute-start.8 = (bf16[3,448,128]{2,1,0:T(8,128)(2,1)S(1)}, bf16[3,448,128]{2,1,0:T(8,128)(2,1)S(1)}, u32[]{:S(2)}, u32[]{:S(2)}) collective-permute-start(bf16[3,448,128]{2,1,0:T(8,128)(2,1)S(1)} %get-tuple-element.15.refs_0_), channel_id=1, source_target_pairs={{0,48},{16,0},{32,16},{48,32},{1,49},{17,1},{33,17},{49,33},{2,50}... | collective-permute-start | bytes 1032200 | tf_op jit(solution)/shard_map/ppermute | solution.py:332
  65.6 15.8 %collective-permute-start.9 = (bf16[3,448,128]{2,1,0:T(8,128)(2,1)S(1)}, bf16[3,448,128]{2,1,0:T(8,128)(2,1)S(1)}, u32[]{:S(2)}, u32[]{:S(2)}) collective-permute-start(bf16[3,448,128]{2,1,0:T(8,128)(2,1)S(1)} %get-tuple-element.15.refs_0_), channel_id=1, source_target_pairs={{0,32},{16,48},{32,0},{48,16},{1,33},{17,49},{33,1},{49,17},{2,34}... | collective-permute-start | bytes 1032200 | tf_op jit(solution)/shard_map/ppermute | solution.py:332
  80.9 22.3 %copy-start.13 = (bf16[3,448,128]{2,1,0:T(8,128)(2,1)}, bf16[3,448,128]{2,1,0:T(8,128)(2,1)S(1)}, u32[]{:S(2)}) copy-start(bf16[3,448,128]{2,1,0:T(8,128)(2,1)S(1)} %collective-permute-done.8.refs_1_) | copy-start | bytes 1032196
  80.9 22.3 %collective-permute-start.5 = (bf16[3,448,128]{2,1,0:T(8,128)(2,1)S(1)}, bf16[3,448,128]{2,1,0:T(8,128)(2,1)S(1)}, u32[]{:S(2)}, u32[]{:S(2)}) collective-permute-start(bf16[3,448,128]{2,1,0:T(8,128)(2,1)S(1)} %slice_bitcast_fusion.1), channel_id=1, source_target_pairs={{0,64},{64,128},{128,192},{192,0},{1,65},{65,129},{129,193},{193,1... | collective-permute-start | bytes 1032200 | tf_op jit(solution)/shard_map/ppermute | solution.py:332
  81.3 21.9 %copy-start.15 = (bf16[3,448,128]{2,1,0:T(8,128)(2,1)}, bf16[3,448,128]{2,1,0:T(8,128)(2,1)S(1)}, u32[]{:S(2)}) copy-start(bf16[3,448,128]{2,1,0:T(8,128)(2,1)S(1)} %collective-permute-done.9.refs_2_) | copy-start | bytes 1032196
  81.3 21.9 %collective-permute-start.6 = (bf16[3,448,128]{2,1,0:T(8,128)(2,1)S(1)}, bf16[3,448,128]{2,1,0:T(8,128)(2,1)}, u32[]{:S(2)}, u32[]{:S(2)}) collective-permute-start(bf16[3,448,128]{2,1,0:T(8,128)(2,1)S(1)} %slice_bitcast_fusion), channel_id=1, source_target_pairs={{0,192},{64,0},{128,64},{192,128},{1,193},{65,1},{129,65},{193,129... | collective-permute-start | bytes 1032200 | tf_op jit(solution)/shard_map/ppermute | solution.py:332
  83.0 0.8 copy-start.24
  83.0 1.1 copy-start.25
  84.1 0.9 copy-start.26
  103.2 1.7 collective-permute-start.10
  103.3 2.5 %collective-permute-start.11 = (bf16[3,448,128]{2,1,0:T(8,128)(2,1)}, bf16[3,448,128]{2,1,0:T(8,128)(2,1)}, u32[]{:S(2)}, u32[]{:S(2)}) collective-permute-start(bf16[3,448,128]{2,1,0:T(8,128)(2,1)} %collective-permute-done.6.refs_8_.refs_4_), channel_id=1, source_target_pairs={{0,1},{1,0},{2,3},{3,2},{4,5},{5,4},{6,7},{7,6},{8,9},{9,8},{10,11... | collective-permute-start | bytes 1032200 | tf_op jit(solution)/shard_map/ppermute | solution.py:332
  103.8 50.0 %collective-permute-start.16 = (bf16[384,3072]{1,0:T(8,128)(2,1)}, bf16[384,3072]{1,0:T(8,128)(2,1)}, u32[]{:S(2)}, u32[]{:S(2)}) collective-permute-start(bf16[384,3072]{1,0:T(8,128)(2,1)} %wv_mine.1), channel_id=1, source_target_pairs={{0,1},{1,0},{2,3},{3,2},{4,5},{5,4},{6,7},{7,6},{8,9},{9,8},{10,11... | collective-permute-start | bytes 7077896 | tf_op jit(solution)/shard_map/ppermute | solution.py:332
  103.9 50.0 %collective-permute-start.17 = (bf16[384,3072]{1,0:T(8,128)(2,1)}, bf16[384,3072]{1,0:T(8,128)(2,1)}, u32[]{:S(2)}, u32[]{:S(2)}) collective-permute-start(bf16[384,3072]{1,0:T(8,128)(2,1)} %wa_mine.1), channel_id=1, source_target_pairs={{0,1},{1,0},{2,3},{3,2},{4,5},{5,4},{6,7},{7,6},{8,9},{9,8},{10,11... | collective-permute-start | bytes 7077896 | tf_op jit(solution)/shard_map/ppermute | solution.py:332
  105.0 0.8 copy-start.17
  105.8 1.0 copy-start.14
  106.8 1.0 copy-start.16
  121.0 19.6 %collective-permute-start.12 = (bf16[1392,128]{1,0:T(8,128)(2,1)}, bf16[1392,128]{1,0:T(8,128)(2,1)S(1)}, u32[]{:S(2)}, u32[]{:S(2)}) collective-permute-start(bf16[1392,128]{1,0:T(8,128)(2,1)} %get-tuple-element.23), channel_id=1, source_target_pairs={{0,48},{16,0},{32,16},{48,32},{1,49},{17,1},{33,17},{49,33},{2,50}... | collective-permute-start | bytes 1069064 | tf_op jit(solution)/shard_map/ppermute | solution.py:332
  124.8 19.1 %collective-permute-start.13 = (bf16[1392,128]{1,0:T(8,128)(2,1)}, bf16[1392,128]{1,0:T(8,128)(2,1)S(1)}, u32[]{:S(2)}, u32[]{:S(2)}) collective-permute-start(bf16[1392,128]{1,0:T(8,128)(2,1)} %get-tuple-element.24), channel_id=1, source_target_pairs={{0,16},{16,32},{32,48},{48,0},{1,17},{17,33},{33,49},{49,1},{2,18}... | collective-permute-start | bytes 1069064 | tf_op jit(solution)/shard_map/ppermute | solution.py:332
  124.8 19.1 %collective-permute-start.14 = (bf16[1392,128]{1,0:T(8,128)(2,1)}, bf16[1392,128]{1,0:T(8,128)(2,1)S(1)}, u32[]{:S(2)}, u32[]{:S(2)}) collective-permute-start(bf16[1392,128]{1,0:T(8,128)(2,1)} %get-tuple-element.25), channel_id=1, source_target_pairs={{0,32},{16,48},{32,0},{48,16},{1,33},{17,49},{33,1},{49,17},{2,34}... | collective-permute-start | bytes 1069064 | tf_op jit(solution)/shard_map/ppermute | solution.py:332
  126.3 1.0 copy-start.18
  143.9 1.0 copy-start.1
  148.3 5.5 %collective-permute-start.15 = (bf16[224,384]{1,0:T(8,128)(2,1)S(1)}, bf16[224,384]{1,0:T(8,128)(2,1)S(1)}, u32[]{:S(2)}, u32[]{:S(2)}) collective-permute-start(bf16[224,384]{1,0:T(8,128)(2,1)S(1)} %get-tuple-element.27), channel_id=1, source_target_pairs={{0,8},{8,0},{1,9},{9,1},{2,10},{10,2},{3,11},{11,3},{4,12},{12,4},... | collective-permute-start | bytes 516104 | tf_op jit(solution)/shard_map/ppermute | solution.py:332
  160.2 3.7 %copy-start.27 = (s32[8]{0:T(128)S(1)}, s32[8]{0:T(128)}, u32[]{:S(2)}) copy-start(s32[8]{0:T(128)} %param.29) | copy-start | bytes 100
  160.3 36.6 %all-to-all-start.1 = ((bf16[4,56,3072]{2,1,0:T(8,128)(2,1)}), bf16[4,56,3072]{2,1,0:T(8,128)(2,1)S(1)}, u32[]{:S(2)}, u32[]{:S(2)}) async-start(bf16[4,56,3072]{2,1,0:T(8,128)(2,1)} %shard_map.182), calls=%async_computation.1 | async-start | bytes 2752512 | tf_op jit(solution)/shard_map/all_to_all | solution.py:434
  164.0 2.1 %copy-start.19 = (bf16[256,3072]{1,0:T(8,128)(2,1)S(1)}, bf16[256,3072]{1,0:T(8,128)(2,1)}, u32[]{:S(2)}) copy-start(bf16[256,3072]{1,0:T(8,128)(2,1)} %param.28) | copy-start | bytes 4718596
  166.1 31.0 %copy-start.20 = (bf16[48,3072]{1,0:T(8,128)(2,1)S(1)}, bf16[48,3072]{1,0:T(8,128)(2,1)}, u32[]{:S(2)}) copy-start(bf16[48,3072]{1,0:T(8,128)(2,1)} %param.23) | copy-start | bytes 884740
  166.8 31.1 %copy-start.23 = (bf16[8,3072]{1,0:T(8,128)(2,1)S(1)}, bf16[8,3072]{1,0:T(8,128)(2,1)}, u32[]{:S(2)}) copy-start(bf16[8,3072]{1,0:T(8,128)(2,1)} %param.24) | copy-start | bytes 147460
